TPU v7x, 32 devices: a whole 2x2x4 slice. The times are simulated.
32 devices in a mesh: cuts: 4 (over z), gx: 2 (over x), gy: 4 (over y, core).
Axes of the slice: x: 2, y: 2, z: 4, core: 2. Of those that a mesh axis runs over, the one named last changes fastest.
Arguments:
- start_heads: float32 [4, 32, 8, 1024], P('cuts', None, 'gx', 'gy'), may hold values from -4 to -0.3
- soil_class: int32 [8, 1024], P('gx', 'gy'), may hold values from 0 to 11
- soil_conductivity: float32 [12], replicated, may hold values from 0.005 to 0.025
- soil_entry: float32 [12], replicated, may hold values from 0.5 to 3
- soil_shape: float32 [12], replicated, may hold values from 1.4 to 2.6
- soil_porosity: float32 [12], replicated, may hold values from 0.25 to 0.45
- emitter_cell: int32 [2048], P(('gx', 'gy')), may hold values from 0 to 1023
- emitter_plan: int32 [2048], P(('gx', 'gy')), may hold values from 0 to 15
- plan_rates: float32 [16, 4], replicated, may hold values from 0.05 to 0.5
Outputs:
- end_heads: float32 [4, 32, 8, 1024], P('cuts', None, 'gx', 'gy')
All inputs are finite; a program needn't handle non-finite values.
Results may differ from a plain program's by a relative error of at most 0.0001.
Values sent between devices are 32-bit elements; how exact they have to be, the bound alone decides.
A program may use at most 64 MiB of HBM per device.

v0:
```python
import jax
import jax.numpy as jnp
from jax import lax
from jax.sharding import PartitionSpec as P

FINE_STEPS = 4
COARSE_STEPS = 2


STORAGE = 0.3


def with_halo(cells, sides, width):
    for axis, dim in sides:
        count = lax.axis_size(axis)
        ends = count - 1
        head = lax.slice_in_dim(cells, 0, width, axis=dim)
        tail = lax.slice_in_dim(cells, cells.shape[dim] - width, cells.shape[dim], axis=dim)
        cells = jnp.concatenate(
            [
                lax.ppermute(tail, axis, [(i, (i + 1) % count) for i in range(ends)]),
                cells,
                lax.ppermute(head, axis, [((i + 1) % count, i) for i in range(ends)]),
            ],
            axis=dim,
        )
    return cells


def from_behind(array, axis, by):
    length = lax.axis_size(axis)
    pairs = [(i, i + by) for i in range(length) if 0 <= i + by < length]
    return lax.ppermute(array, axis, pairs)


def conductivity(heads, saturated, entry_scale, shape_index):
    exponent = 1.0 - 1.0 / shape_index
    suction = jnp.maximum(-heads, 0.0) * entry_scale
    powered = jnp.power(suction, shape_index)
    wetted = powered / (1.0 + powered)
    return (
        saturated
        * jnp.sqrt(jnp.power(1.0 + powered, -exponent))
        * jnp.square(1.0 - jnp.power(wetted, exponent))
    )


def capacity(heads, entry_scale, shape_index, porosity):
    exponent = 1.0 - 1.0 / shape_index
    suction = jnp.maximum(-heads, 0.0) * entry_scale
    powered = jnp.power(suction, shape_index)
    return STORAGE + porosity * exponent * shape_index * entry_scale * jnp.power(
        suction, shape_index - 1.0
    ) * jnp.power(1.0 + powered, -exponent - 1.0)


def open_faces(rows, columns):
    global_row = lax.axis_index("gx") * rows + jnp.arange(rows, dtype=jnp.int32)
    global_column = lax.axis_index("gy") * columns + jnp.arange(columns, dtype=jnp.int32)
    row_total = lax.axis_size("gx") * rows
    column_total = lax.axis_size("gy") * columns
    return (
        (global_row + 1 < row_total)[None, :, None],
        (global_row > 0)[None, :, None],
        (global_column + 1 < column_total)[None, None, :],
        (global_column > 0)[None, None, :],
    )


def advance_local(
    heads, padded, conduct, conduct_pad, storage_term, source, spacing, interval, faces
):
    row_up, row_down, column_up, column_down = faces
    inverse = 1.0 / (spacing * spacing)
    flow_up = jnp.where(
        row_up,
        0.5 * (conduct + conduct_pad[:, 2:, 1:-1]) * (padded[:, 2:, 1:-1] - heads) * inverse,
        0.0,
    )
    flow_down = jnp.where(
        row_down,
        0.5 * (conduct + conduct_pad[:, :-2, 1:-1]) * (padded[:, :-2, 1:-1] - heads) * inverse,
        0.0,
    )
    balance_x = flow_up + flow_down
    flow_right = jnp.where(
        column_up,
        0.5 * (conduct + conduct_pad[:, 1:-1, 2:]) * (padded[:, 1:-1, 2:] - heads) * inverse,
        0.0,
    )
    flow_left = jnp.where(
        column_down,
        0.5 * (conduct + conduct_pad[:, 1:-1, :-2]) * (padded[:, 1:-1, :-2] - heads) * inverse,
        0.0,
    )
    balance_y = flow_right + flow_left
    downward = 0.5 * (conduct[:-1] + conduct[1:]) * ((heads[:-1] - heads[1:]) / spacing + 1.0)
    inflow = jnp.concatenate([source[None], downward], axis=0)
    outflow = jnp.concatenate([downward, conduct[-1:]], axis=0)
    balance = balance_x + balance_y + (inflow - outflow) / spacing
    return heads + interval * balance / storage_term


def run_steps(heads, params, source, faces, count, spacing, interval, is_fine):
    for s in range(count):
        conduct = conductivity(heads, params[0], params[1], params[2])
        storage_term = capacity(heads, params[1], params[2], params[3])
        stacked = jnp.stack([heads, conduct])
        if is_fine:
            stacked = with_halo(stacked, (("gx", 2), ("gy", 3)), 1)
        else:
            stacked = with_halo(stacked, (("gx", 2), ("gy", 3)), 1)
        padded = stacked[0]
        conduct_pad = stacked[1]
        heads = advance_local(
            heads, padded, conduct, conduct_pad, storage_term, source, spacing, interval, faces
        )
    return heads


def restrict(field):
    depth, rows, columns = field.shape
    return field.reshape(depth // 2, 2, rows // 2, 2, columns // 2, 2).mean(axis=(1, 3, 5))


def prolong(field):
    return jnp.repeat(jnp.repeat(jnp.repeat(field, 2, axis=0), 2, axis=1), 2, axis=2)


def coarsen_columns(params):
    count, rows, columns = params.shape
    return params.reshape(count, rows // 2, 2, columns // 2, 2).mean(axis=(2, 4))


def on_device(
    start_heads,
    soil_class,
    soil_conductivity,
    soil_entry,
    soil_shape,
    soil_porosity,
    emitter_cell,
    emitter_plan,
    plan_rates,
):
    heads_start = start_heads[0]
    depth, rows, columns = heads_start.shape
    table = jnp.stack([soil_conductivity, soil_entry, soil_shape, soil_porosity])
    classes = jnp.arange(table.shape[1], dtype=jnp.int32)
    matches = soil_class[None, :, :] == classes[:, None, None]
    params = jnp.sum(jnp.where(matches[None], table[:, :, None, None], 0.0), axis=1)
    coarse_params = coarsen_columns(params)
    plans = jnp.arange(plan_rates.shape[0], dtype=jnp.int32)
    picks = emitter_plan[:, None] == plans[None, :]
    rates_all = jnp.sum(jnp.where(picks[:, :, None], plan_rates[None], 0.0), axis=1)
    slice_total = rates_all.shape[1]
    sources = (
        jnp.zeros((slice_total, rows * columns), jnp.float32)
        .at[:, emitter_cell]
        .add(rates_all.T)
        .reshape(slice_total, rows, columns)
    )
    coarse_sources = coarsen_columns(sources)
    slice_index = lax.axis_index("cuts")
    slice_count = lax.axis_size("cuts")
    source = sources[slice_index]
    coarse_source = coarse_sources[slice_index]
    fine_open = open_faces(rows, columns)
    coarse_open = open_faces(rows // 2, columns // 2)
    fine_heads = run_steps(heads_start, params, source, fine_open, FINE_STEPS, 1.0, 1.0, True)

    def coarse_run(current, coarse_src):
        return run_steps(
            current, coarse_params, coarse_src, coarse_open, COARSE_STEPS, 2.0, 2.0, False
        )

    coarse_start = restrict(heads_start)
    coarse_old = coarse_run(coarse_start, coarse_source)
    correction = restrict(fine_heads) - coarse_old
    current = coarse_start
    coarse_new = coarse_old
    for s in range(slice_count):
        coarse_new = coarse_run(current, coarse_source)
        if s + 1 < slice_count:
            arrived = from_behind(coarse_new + correction, "cuts", 1)
            current = jnp.where(slice_index == 0, coarse_start, arrived)
    end_state = fine_heads + prolong(coarse_new - coarse_old)
    return end_state[None]


def solution(mesh):
    in_specs = (
        P("cuts", None, "gx", "gy"),
        P("gx", "gy"),
        P(),
        P(),
        P(),
        P(),
        P(("gx", "gy")),
        P(("gx", "gy")),
        P(),
    )
    out_specs = P("cuts", None, "gx", "gy")
    return jax.shard_map(
        on_device, mesh=mesh, in_specs=in_specs, out_specs=out_specs, check_vma=False
    )
```

profile of v0, /device:TPU:16, one launch (start us, length us, event | category | flops | bytes accessed | tf_op | source)
XLA Modules:
  0.0 297.7 jit_solution(16239975555570123671)
XLA Ops:
  3.7 3.4 %collective-permute-start = (f32[2,32,1,256]{3,1,2,0:T(8,128)S(1)}, f32[2,32,1,256]{3,1,2,0:T(8,128)S(1)}, u32[]{:S(2)}, u32[]{:S(2)}) collective-permute-start(f32[2,32,1,256]{3,1,2,0:T(8,128)S(1)} %get-tuple-element.57), channel_id=1, source_target_pairs={{0,4},{1,5},{2,6},{3,7},{8,12},{9,13},{10,14},{11,15},{16,20},{17,... | collective-permute-start | bytes 196616 | tf_op jit(solution)/shard_map/ppermute | solution.py:21
  8.7 9.8 %reshape_squeeze.3 = f32[16,2,2,2,128,2]{5,4,1,0,3,2:T(8,128)} reshape(f32[1,32,4,256]{3,1,2,0:T(8,128)S(1)} %get-tuple-element.75) | data formatting | bytes 262144 | tf_op jit(solution)/shard_map/reshape;squeeze | solution.py:123
  19.5 4.1 %reduce_sum.56 = f32[16,2,128]{2,0,1:T(8,128)S(1)} reduce(f32[16,2,2,2,128,2]{5,4,1,0,3,2:T(8,128)} %reshape_squeeze.3, f32[]{:T(128)} %constant.34.clone.1), dimensions={1,3,5}, to_apply=%region_3.4 | reduce | flops 28672 | bytes 147460 | tf_op jit(solution)/shard_map/reduce_sum | solution.py:123
  23.8 4.5 %collective-permute-start.16 = (f32[2,16,1,128]{3,1,2,0:T(8,128)S(1)}, f32[2,16,1,128]{3,1,2,0:T(8,128)S(1)}, u32[]{:S(2)}, u32[]{:S(2)}) collective-permute-start(f32[2,16,1,128]{3,1,2,0:T(8,128)S(1)} %get-tuple-element.107), channel_id=1, source_target_pairs={{0,4},{1,5},{2,6},{3,7},{8,12},{9,13},{10,14},{11,15},{16,20},{17,... | collective-permute-start | bytes 49160 | tf_op jit(solution)/shard_map/ppermute | solution.py:21
  30.8 1.6 scatter_custom_fusion
  33.1 3.2 %fusion.2 = f32[32,4,256]{0,2,1:T(8,128)S(1)} fusion(f32[1,32,4,256]{1,3,2,0:T(8,128)S(1)} %copy.92, f32[4,256]{1,0:T(4,128)S(1)} %get-tuple-element.113, f32[4,256]{1,0:T(4,128)S(1)} %get-tuple-element.115, f32[4,256]{1,0:T(4,128)S(1)} %get-tuple-element.117, f32[4,256]{1,0:T(4,128)S(1)} %get-tuple-element.118, f32[4,256]{1,0:T(4,128)S(1)} %get-tuple-element.119), kind=kLoop, calls=%fused_computation.19 | loop fusion | flops 294912 | bytes 282624 | tf_op jit(solution)/shard_map/mul | solution.py:42
  41.9 2.5 collective-permute-done.19
  46.0 4.5 %collective-permute-start.20 = (f32[2,16,1,128]{3,1,2,0:T(8,128)S(1)}, f32[2,16,1,128]{3,1,2,0:T(8,128)S(1)}, u32[]{:S(2)}, u32[]{:S(2)}) collective-permute-start(f32[2,16,1,128]{3,1,2,0:T(8,128)S(1)} %get-tuple-element.105), channel_id=1, source_target_pairs={{0,4},{1,5},{2,6},{3,7},{8,12},{9,13},{10,14},{11,15},{16,20},{17,... | collective-permute-start | bytes 49160 | tf_op jit(solution)/shard_map/ppermute | solution.py:21
  52.0 4.6 %collective-permute-start.2 = (f32[2,32,6,1]{3,1,2,0:T(8,128)S(1)}, f32[2,32,6,1]{3,1,2,0:T(8,128)S(1)}, u32[]{:S(2)}, u32[]{:S(2)}) collective-permute-start(f32[2,32,6,1]{3,1,2,0:T(8,128)S(1)} %get-tuple-element.49), channel_id=1, source_target_pairs={{0,1},{1,2},{2,3},{4,5},{5,6},{6,7},{8,9},{9,10},{10,11},{12,13},{... | collective-permute-start | bytes 4616 | tf_op jit(solution)/shard_map/ppermute | solution.py:21
  58.1 1.8 collective-permute-done.3
  60.9 10.2 %fusion.12 = (f32[32,4,256]{0,2,1:T(8,128)}, f32[32,4,256]{0,2,1:T(8,128)S(1)}) fusion(f32[4,256]{1,0:T(4,128)S(1)} %get-tuple-element.113, f32[4,256]{1,0:T(4,128)S(1)} %get-tuple-element.115, f32[4,256]{1,0:T(4,128)S(1)} %get-tuple-element.117, f32[4,256]{1,0:T(4,128)S(1)} %get-tuple-element.118, f32[4,256]{1,0:T(4,128)S(1)} %get-tuple-element.119, ...), kind=kLoop, calls=%fused_computation.29 | loop fusion | flops 1638400 | bytes 1610248 | tf_op jit(solution)/shard_map/mul | solution.py:42
  71.1 3.2 %fusion.467 = f32[1,32,4,256]{1,3,2,0:T(8,128)S(1)} fusion(f32[4,256]{1,0:T(4,128)S(1)} %get-tuple-element.113, f32[4,256]{1,0:T(4,128)S(1)} %get-tuple-element.115, f32[4,256]{1,0:T(4,128)S(1)} %get-tuple-element.117, f32[4,256]{1,0:T(4,128)S(1)} %get-tuple-element.118, f32[32,4,256]{0,2,1:T(8,128)S(1)} %get-tuple-element.34, ...), kind=kLoop, calls=%fused_computation.763 | loop fusion | flops 294912 | bytes 282624 | tf_op jit(solution)/shard_map/stack | solution.py:108
  74.7 4.3 %collective-permute-start.4 = (f32[2,32,1,256]{3,1,2,0:T(8,128)S(1)}, f32[2,32,1,256]{3,1,2,0:T(8,128)S(1)}, u32[]{:S(2)}, u32[]{:S(2)}) collective-permute-start(f32[2,32,1,256]{3,1,2,0:T(8,128)S(1)} %get-tuple-element.55), channel_id=1, source_target_pairs={{0,4},{1,5},{2,6},{3,7},{8,12},{9,13},{10,14},{11,15},{16,20},{17,... | collective-permute-start | bytes 196616 | tf_op jit(solution)/shard_map/ppermute | solution.py:21
  81.0 5.8 %collective-permute-start.22 = (f32[2,16,4,1]{3,1,2,0:T(8,128)}, f32[2,16,4,1]{3,1,2,0:T(8,128)S(1)}, u32[]{:S(2)}, u32[]{:S(2)}) collective-permute-start(f32[2,16,4,1]{3,1,2,0:T(8,128)} %get-tuple-element.89), channel_id=1, source_target_pairs={{0,1},{1,2},{2,3},{4,5},{5,6},{6,7},{8,9},{9,10},{10,11},{12,13},{... | collective-permute-start | bytes 1544 | tf_op jit(solution)/shard_map/ppermute | solution.py:21
  88.3 3.0 %collective-permute-start.6 = (f32[2,32,6,1]{3,1,2,0:T(8,128)S(1)}, f32[2,32,6,1]{3,1,2,0:T(8,128)S(1)}, u32[]{:S(2)}, u32[]{:S(2)}) collective-permute-start(f32[2,32,6,1]{3,1,2,0:T(8,128)S(1)} %get-tuple-element.47), channel_id=1, source_target_pairs={{0,1},{1,2},{2,3},{4,5},{5,6},{6,7},{8,9},{9,10},{10,11},{12,13},{... | collective-permute-start | bytes 4616 | tf_op jit(solution)/shard_map/ppermute | solution.py:21
  92.6 2.3 fusion.79
  95.0 2.0 slice.1097
  97.9 10.1 %fusion.22 = (f32[32,4,256]{0,2,1:T(8,128)}, f32[32,4,256]{0,2,1:T(8,128)S(1)}) fusion(f32[4,256]{1,0:T(4,128)S(1)} %get-tuple-element.113, f32[4,256]{1,0:T(4,128)S(1)} %get-tuple-element.115, f32[4,256]{1,0:T(4,128)S(1)} %get-tuple-element.117, f32[4,256]{1,0:T(4,128)S(1)} %get-tuple-element.118, f32[4,256]{1,0:T(4,128)S(1)} %get-tuple-element.119, ...), kind=kLoop, calls=%fused_computation.39 | loop fusion | flops 1638400 | bytes 1610248 | tf_op jit(solution)/shard_map/mul | solution.py:42
  108.1 3.2 %fusion.466 = f32[1,32,4,256]{1,3,2,0:T(8,128)S(1)} fusion(f32[4,256]{1,0:T(4,128)S(1)} %get-tuple-element.113, f32[4,256]{1,0:T(4,128)S(1)} %get-tuple-element.115, f32[4,256]{1,0:T(4,128)S(1)} %get-tuple-element.117, f32[4,256]{1,0:T(4,128)S(1)} %get-tuple-element.118, f32[32,4,256]{0,2,1:T(8,128)S(1)} %get-tuple-element.32, ...), kind=kLoop, calls=%fused_computation.762 | loop fusion | flops 294912 | bytes 282624 | tf_op jit(solution)/shard_map/stack | solution.py:108
  111.7 4.3 %collective-permute-start.8 = (f32[2,32,1,256]{3,1,2,0:T(8,128)S(1)}, f32[2,32,1,256]{3,1,2,0:T(8,128)S(1)}, u32[]{:S(2)}, u32[]{:S(2)}) collective-permute-start(f32[2,32,1,256]{3,1,2,0:T(8,128)S(1)} %get-tuple-element.53), channel_id=1, source_target_pairs={{0,4},{1,5},{2,6},{3,7},{8,12},{9,13},{10,14},{11,15},{16,20},{17,... | collective-permute-start | bytes 196616 | tf_op jit(solution)/shard_map/ppermute | solution.py:21
  118.2 3.9 %collective-permute-done.9 = f32[2,32,1,256]{3,1,2,0:T(8,128)S(1)} collective-permute-done((f32[2,32,1,256]{3,1,2,0:T(8,128)S(1)}, f32[2,32,1,256]{3,1,2,0:T(8,128)S(1)}, u32[]{:S(2)}, u32[]{:S(2)}) %collective-permute-start.9) | collective-permute-done | bytes 65568 | tf_op jit(solution)/shard_map/ppermute | solution.py:23
  122.2 3.4 %collective-permute-start.10 = (f32[2,32,6,1]{3,1,2,0:T(8,128)S(1)}, f32[2,32,6,1]{3,1,2,0:T(8,128)S(1)}, u32[]{:S(2)}, u32[]{:S(2)}) collective-permute-start(f32[2,32,6,1]{3,1,2,0:T(8,128)S(1)} %get-tuple-element.45), channel_id=1, source_target_pairs={{0,1},{1,2},{2,3},{4,5},{5,6},{6,7},{8,9},{9,10},{10,11},{12,13},{... | collective-permute-start | bytes 4616 | tf_op jit(solution)/shard_map/ppermute | solution.py:21
  127.2 2.4 fusion.60
  129.6 2.0 slice.1114
  132.5 10.1 %fusion.32 = (f32[32,4,256]{0,2,1:T(8,128)}, f32[32,4,256]{0,2,1:T(8,128)S(1)}) fusion(f32[4,256]{1,0:T(4,128)S(1)} %get-tuple-element.113, f32[4,256]{1,0:T(4,128)S(1)} %get-tuple-element.115, f32[4,256]{1,0:T(4,128)S(1)} %get-tuple-element.117, f32[4,256]{1,0:T(4,128)S(1)} %get-tuple-element.118, f32[4,256]{1,0:T(4,128)S(1)} %get-tuple-element.119, ...), kind=kLoop, calls=%fused_computation.49 | loop fusion | flops 1638400 | bytes 1610248 | tf_op jit(solution)/shard_map/mul | solution.py:42
  142.7 3.2 %fusion.465 = f32[1,32,4,256]{1,3,2,0:T(8,128)S(1)} fusion(f32[4,256]{1,0:T(4,128)S(1)} %get-tuple-element.113, f32[4,256]{1,0:T(4,128)S(1)} %get-tuple-element.115, f32[4,256]{1,0:T(4,128)S(1)} %get-tuple-element.117, f32[4,256]{1,0:T(4,128)S(1)} %get-tuple-element.118, f32[32,4,256]{0,2,1:T(8,128)S(1)} %get-tuple-element.30, ...), kind=kLoop, calls=%fused_computation.761 | loop fusion | flops 294912 | bytes 282624 | tf_op jit(solution)/shard_map/stack | solution.py:108
  146.3 1.9 collective-permute-start.12
  150.0 4.3 %collective-permute-done.13 = f32[2,32,1,256]{3,1,2,0:T(8,128)S(1)} collective-permute-done((f32[2,32,1,256]{3,1,2,0:T(8,128)S(1)}, f32[2,32,1,256]{3,1,2,0:T(8,128)S(1)}, u32[]{:S(2)}, u32[]{:S(2)}) %collective-permute-start.13) | collective-permute-done | bytes 65568 | tf_op jit(solution)/shard_map/ppermute | solution.py:23
  154.4 3.7 %collective-permute-start.14 = (f32[2,32,6,1]{3,1,2,0:T(8,128)S(1)}, f32[2,32,6,1]{3,1,2,0:T(8,128)S(1)}, u32[]{:S(2)}, u32[]{:S(2)}) collective-permute-start(f32[2,32,6,1]{3,1,2,0:T(8,128)S(1)} %get-tuple-element.43), channel_id=1, source_target_pairs={{0,1},{1,2},{2,3},{4,5},{5,6},{6,7},{8,9},{9,10},{10,11},{12,13},{... | collective-permute-start | bytes 4616 | tf_op jit(solution)/shard_map/ppermute | solution.py:21
  159.5 2.4 fusion.41
  161.8 2.0 slice.1131
  164.8 7.0 %fusion.39 = f32[32,4,256]{0,2,1:T(8,128)S(1)} fusion(f32[32,4,256]{0,2,1:T(8,128)S(1)} %get-tuple-element.30, f32[32,6,258]{0,2,1:T(8,128)S(1)} %bitcast.122, f32[32,6,258]{0,2,1:T(8,128)S(1)} %bitcast.121, f32[31,4,256]{0,2,1:T(8,128)} %fusion.41, f32[1,4,256]{0,2,1:T(8,128)} %slice.1131, f32[1,4,256]{0,2,1:T(8,128)S(1)} %constant_dynamic-slice_fusion, ...), kind=kLoop, calls=%fused_computation.56 | loop fusion | flops 1343488 | bytes 1479176 | tf_op jit(solution)/shard_map/add | solution.py:101
  172.1 9.8 %reshape.140 = f32[16,2,2,2,128,2]{5,4,1,0,3,2:T(8,128)} reshape(f32[32,4,256]{2,0,1:T(8,128)S(1)} %copy.116) | data formatting | bytes 262144 | tf_op jit(solution)/shard_map/reshape | solution.py:123
  181.9 4.0 %reduce_sum.59 = f32[16,2,128]{2,0,1:T(8,128)S(1)} reduce(f32[16,2,2,2,128,2]{5,4,1,0,3,2:T(8,128)} %reshape.140, f32[]{:T(128)} %constant.34.clone.1), dimensions={1,3,5}, to_apply=%region_6.7 | reduce | flops 28672 | bytes 147460 | tf_op jit(solution)/shard_map/reduce_sum | solution.py:123
  186.2 3.5 %collective-permute-start.24 = (f32[16,2,128]{2,0,1:T(8,128)S(1)}, f32[16,2,128]{2,0,1:T(8,128)S(1)}, u32[]{:S(2)}, u32[]{:S(2)}) collective-permute-start(f32[16,2,128]{2,0,1:T(8,128)S(1)} %get-tuple-element.25), channel_id=1, source_target_pairs={{0,8},{8,16},{16,24},{1,9},{9,17},{17,25},{2,10},{10,18},{18,26},{... | collective-permute-start | bytes 49160 | tf_op jit(solution)/shard_map/ppermute | solution.py:33
  189.7 2.1 collective-permute-done.24
  191.9 1.9 collective-permute-start.25
  195.2 4.2 %collective-permute-done.26 = f32[2,16,1,128]{3,1,2,0:T(8,128)S(1)} collective-permute-done((f32[2,16,1,128]{3,1,2,0:T(8,128)S(1)}, f32[2,16,1,128]{3,1,2,0:T(8,128)S(1)}, u32[]{:S(2)}, u32[]{:S(2)}) %collective-permute-start.26) | collective-permute-done | bytes 16416 | tf_op jit(solution)/shard_map/ppermute | solution.py:23
  199.5 3.0 %collective-permute-start.27 = (f32[2,16,4,1]{3,1,2,0:T(8,128)S(1)}, f32[2,16,4,1]{3,1,2,0:T(8,128)S(1)}, u32[]{:S(2)}, u32[]{:S(2)}) collective-permute-start(f32[2,16,4,1]{3,1,2,0:T(8,128)S(1)} %get-tuple-element.87), channel_id=1, source_target_pairs={{0,1},{1,2},{2,3},{4,5},{5,6},{6,7},{8,9},{9,10},{10,11},{12,13},{... | collective-permute-start | bytes 1544 | tf_op jit(solution)/shard_map/ppermute | solution.py:21
  203.9 5.0 %collective-permute-done.28 = f32[2,16,4,1]{3,1,2,0:T(8,128)S(1)} collective-permute-done((f32[2,16,4,1]{3,1,2,0:T(8,128)S(1)}, f32[2,16,4,1]{3,1,2,0:T(8,128)S(1)}, u32[]{:S(2)}, u32[]{:S(2)}) %collective-permute-start.28) | collective-permute-done | bytes 544 | tf_op jit(solution)/shard_map/ppermute | solution.py:23
  209.3 1.6 collective-permute-start.29
  212.3 4.2 %collective-permute-done.30 = f32[2,16,1,128]{3,1,2,0:T(8,128)S(1)} collective-permute-done((f32[2,16,1,128]{3,1,2,0:T(8,128)S(1)}, f32[2,16,1,128]{3,1,2,0:T(8,128)S(1)}, u32[]{:S(2)}, u32[]{:S(2)}) %collective-permute-start.30) | collective-permute-done | bytes 16416 | tf_op jit(solution)/shard_map/ppermute | solution.py:23
  216.6 3.4 %collective-permute-start.31 = (f32[2,16,4,1]{3,1,2,0:T(8,128)S(1)}, f32[2,16,4,1]{3,1,2,0:T(8,128)S(1)}, u32[]{:S(2)}, u32[]{:S(2)}) collective-permute-start(f32[2,16,4,1]{3,1,2,0:T(8,128)S(1)} %get-tuple-element.85), channel_id=1, source_target_pairs={{0,1},{1,2},{2,3},{4,5},{5,6},{6,7},{8,9},{9,10},{10,11},{12,13},{... | collective-permute-start | bytes 1544 | tf_op jit(solution)/shard_map/ppermute | solution.py:21
  221.4 2.7 collective-permute-done.32
  224.4 3.7 %collective-permute-start.33 = (f32[16,2,128]{2,0,1:T(8,128)S(1)}, f32[16,2,128]{2,0,1:T(8,128)S(1)}, u32[]{:S(2)}, u32[]{:S(2)}) collective-permute-start(f32[16,2,128]{2,0,1:T(8,128)S(1)} %fusion.173), channel_id=1, source_target_pairs={{0,8},{8,16},{16,24},{1,9},{9,17},{17,25},{2,10},{10,18},{18,26},{... | collective-permute-start | bytes 49160 | tf_op jit(solution)/shard_map/ppermute | solution.py:33
  228.1 1.9 collective-permute-done.33
  230.1 1.6 collective-permute-start.34
  233.2 4.2 %collective-permute-done.35 = f32[2,16,1,128]{3,1,2,0:T(8,128)S(1)} collective-permute-done((f32[2,16,1,128]{3,1,2,0:T(8,128)S(1)}, f32[2,16,1,128]{3,1,2,0:T(8,128)S(1)}, u32[]{:S(2)}, u32[]{:S(2)}) %collective-permute-start.35) | collective-permute-done | bytes 16416 | tf_op jit(solution)/shard_map/ppermute | solution.py:23
  237.5 2.3 collective-permute-start.36
  241.1 3.9 %collective-permute-done.37 = f32[2,16,4,1]{3,1,2,0:T(8,128)S(1)} collective-permute-done((f32[2,16,4,1]{3,1,2,0:T(8,128)S(1)}, f32[2,16,4,1]{3,1,2,0:T(8,128)S(1)}, u32[]{:S(2)}, u32[]{:S(2)}) %collective-permute-start.37) | collective-permute-done | bytes 544 | tf_op jit(solution)/shard_map/ppermute | solution.py:23
  245.3 1.6 collective-permute-start.38
  248.4 4.2 %collective-permute-done.39 = f32[2,16,1,128]{3,1,2,0:T(8,128)S(1)} collective-permute-done((f32[2,16,1,128]{3,1,2,0:T(8,128)S(1)}, f32[2,16,1,128]{3,1,2,0:T(8,128)S(1)}, u32[]{:S(2)}, u32[]{:S(2)}) %collective-permute-start.39) | collective-permute-done | bytes 16416 | tf_op jit(solution)/shard_map/ppermute | solution.py:23
  252.7 3.4 %collective-permute-start.40 = (f32[2,16,4,1]{3,1,2,0:T(8,128)S(1)}, f32[2,16,4,1]{3,1,2,0:T(8,128)S(1)}, u32[]{:S(2)}, u32[]{:S(2)}) collective-permute-start(f32[2,16,4,1]{3,1,2,0:T(8,128)S(1)} %get-tuple-element.81), channel_id=1, source_target_pairs={{0,1},{1,2},{2,3},{4,5},{5,6},{6,7},{8,9},{9,10},{10,11},{12,13},{... | collective-permute-start | bytes 1544 | tf_op jit(solution)/shard_map/ppermute | solution.py:21
  257.4 2.7 collective-permute-done.41
  260.4 3.5 %collective-permute-start.42 = (f32[16,2,128]{2,0,1:T(8,128)S(1)}, f32[16,2,128]{2,0,1:T(8,128)S(1)}, u32[]{:S(2)}, u32[]{:S(2)}) collective-permute-start(f32[16,2,128]{2,0,1:T(8,128)S(1)} %fusion.194), channel_id=1, source_target_pairs={{0,8},{8,16},{16,24},{1,9},{9,17},{17,25},{2,10},{10,18},{18,26},{... | collective-permute-start | bytes 49160 | tf_op jit(solution)/shard_map/ppermute | solution.py:33
  263.9 2.1 collective-permute-done.42
  266.1 1.6 collective-permute-start.43
  269.2 4.2 %collective-permute-done.44 = f32[2,16,1,128]{3,1,2,0:T(8,128)S(1)} collective-permute-done((f32[2,16,1,128]{3,1,2,0:T(8,128)S(1)}, f32[2,16,1,128]{3,1,2,0:T(8,128)S(1)}, u32[]{:S(2)}, u32[]{:S(2)}) %collective-permute-start.44) | collective-permute-done | bytes 16416 | tf_op jit(solution)/shard_map/ppermute | solution.py:23
  273.5 2.3 collective-permute-start.45
  277.1 3.9 %collective-permute-done.46 = f32[2,16,4,1]{3,1,2,0:T(8,128)S(1)} collective-permute-done((f32[2,16,4,1]{3,1,2,0:T(8,128)S(1)}, f32[2,16,4,1]{3,1,2,0:T(8,128)S(1)}, u32[]{:S(2)}, u32[]{:S(2)}) %collective-permute-start.46) | collective-permute-done | bytes 544 | tf_op jit(solution)/shard_map/ppermute | solution.py:23
  281.3 1.6 collective-permute-start.47
  284.4 4.2 %collective-permute-done.48 = f32[2,16,1,128]{3,1,2,0:T(8,128)S(1)} collective-permute-done((f32[2,16,1,128]{3,1,2,0:T(8,128)S(1)}, f32[2,16,1,128]{3,1,2,0:T(8,128)S(1)}, u32[]{:S(2)}, u32[]{:S(2)}) %collective-permute-start.48) | collective-permute-done | bytes 16416 | tf_op jit(solution)/shard_map/ppermute | solution.py:23
  288.7 3.4 %collective-permute-start.49 = (f32[2,16,4,1]{3,1,2,0:T(8,128)S(1)}, f32[2,16,4,1]{3,1,2,0:T(8,128)S(1)}, u32[]{:S(2)}, u32[]{:S(2)}) collective-permute-start(f32[2,16,4,1]{3,1,2,0:T(8,128)S(1)} %get-tuple-element.77), channel_id=1, source_target_pairs={{0,1},{1,2},{2,3},{4,5},{5,6},{6,7},{8,9},{9,10},{10,11},{12,13},{... | collective-permute-start | bytes 1544 | tf_op jit(solution)/shard_map/ppermute | solution.py:21
  293.5 2.7 collective-permute-done.50
  (247 shorter events, 56.6 us)
Async XLA Ops:
  3.7 48.1 %collective-permute-start = (f32[2,32,1,256]{3,1,2,0:T(8,128)S(1)}, f32[2,32,1,256]{3,1,2,0:T(8,128)S(1)}, u32[]{:S(2)}, u32[]{:S(2)}) collective-permute-start(f32[2,32,1,256]{3,1,2,0:T(8,128)S(1)} %get-tuple-element.57), channel_id=1, source_target_pairs={{0,4},{1,5},{2,6},{3,7},{8,12},{9,13},{10,14},{11,15},{16,20},{17,... | collective-permute-start | bytes 196616 | tf_op jit(solution)/shard_map/ppermute | solution.py:21
  7.1 44.7 %collective-permute-start.1 = (f32[2,32,1,256]{3,1,2,0:T(8,128)S(1)}, f32[2,32,1,256]{3,1,2,0:T(8,128)S(1)}, u32[]{:S(2)}, u32[]{:S(2)}) collective-permute-start(f32[2,32,1,256]{3,1,2,0:T(8,128)S(1)} %get-tuple-element.58), channel_id=1, source_target_pairs={{4,0},{5,1},{6,2},{7,3},{12,8},{13,9},{14,10},{15,11},{20,16},{21,... | collective-permute-start | bytes 196616 | tf_op jit(solution)/shard_map/ppermute | solution.py:23
  8.6 21.8 %copy-start.27 = (s32[256]{0:T(256)S(1)}, s32[256]{0:T(256)}, u32[]{:S(2)}) copy-start(s32[256]{0:T(256)} %param.15) | copy-start | bytes 3076
  8.7 21.8 %copy-start.26 = (s32[256]{0:T(256)S(1)}, s32[256]{0:T(256)}, u32[]{:S(2)}) copy-start(s32[256]{0:T(256)} %param.16) | copy-start | bytes 3076
  8.7 21.8 %copy-start.25 = (f32[16,4]{0,1:T(4,128)S(1)}, f32[16,4]{0,1:T(4,128)}, u32[]{:S(2)}) copy-start(f32[16,4]{0,1:T(4,128)} %param.17) | copy-start | bytes 772
  19.5 25.1 %copy-start.2 = (f32[2,128]{1,0:T(2,128)}, f32[2,128]{1,0:T(2,128)S(1)}, u32[]{:S(2)}) copy-start(f32[2,128]{1,0:T(2,128)S(1)} %get-tuple-element.5) | copy-start | bytes 3076
  19.5 25.1 %copy-start.4 = (f32[2,128]{1,0:T(2,128)}, f32[2,128]{1,0:T(2,128)S(1)}, u32[]{:S(2)}) copy-start(f32[2,128]{1,0:T(2,128)S(1)} %get-tuple-element.7) | copy-start | bytes 3076
  19.5 25.1 %copy-start.6 = (f32[2,128]{1,0:T(2,128)}, f32[2,128]{1,0:T(2,128)S(1)}, u32[]{:S(2)}) copy-start(f32[2,128]{1,0:T(2,128)S(1)} %get-tuple-element.9) | copy-start | bytes 3076
  23.8 14.3 %collective-permute-start.16 = (f32[2,16,1,128]{3,1,2,0:T(8,128)S(1)}, f32[2,16,1,128]{3,1,2,0:T(8,128)S(1)}, u32[]{:S(2)}, u32[]{:S(2)}) collective-permute-start(f32[2,16,1,128]{3,1,2,0:T(8,128)S(1)} %get-tuple-element.107), channel_id=1, source_target_pairs={{0,4},{1,5},{2,6},{3,7},{8,12},{9,13},{10,14},{11,15},{16,20},{17,... | collective-permute-start | bytes 49160 | tf_op jit(solution)/shard_map/ppermute | solution.py:21
  28.3 9.8 %collective-permute-start.17 = (f32[2,16,1,128]{3,1,2,0:T(8,128)S(1)}, f32[2,16,1,128]{3,1,2,0:T(8,128)S(1)}, u32[]{:S(2)}, u32[]{:S(2)}) collective-permute-start(f32[2,16,1,128]{3,1,2,0:T(8,128)S(1)} %get-tuple-element.108), channel_id=1, source_target_pairs={{4,0},{5,1},{6,2},{7,3},{12,8},{13,9},{14,10},{15,11},{20,16},{21,... | collective-permute-start | bytes 49160 | tf_op jit(solution)/shard_map/ppermute | solution.py:23
  30.5 29.5 %copy-start.11 = (pred[2]{0:T(512)(128)(4,1)}, pred[2]{0:T(512)(128)(4,1)S(1)}, u32[]{:S(2)}) copy-start(pred[2]{0:T(512)(128)(4,1)S(1)} %get-tuple-element.126) | copy-start | bytes 10
  30.5 29.5 %copy-start.13 = (pred[2]{0:T(512)(128)(4,1)}, pred[2]{0:T(512)(128)(4,1)S(1)}, u32[]{:S(2)}) copy-start(pred[2]{0:T(512)(128)(4,1)S(1)} %get-tuple-element.127) | copy-start | bytes 10
  32.3 28.5 %copy-start.19 = (pred[4]{0:T(512)(128)(4,1)S(1)}, pred[4]{0:T(512)(128)(4,1)}, u32[]{:S(2)}) copy-start(pred[4]{0:T(512)(128)(4,1)} %get-tuple-element.122) | copy-start | bytes 16
  32.3 28.5 %copy-start.20 = (pred[4]{0:T(512)(128)(4,1)S(1)}, pred[4]{0:T(512)(128)(4,1)}, u32[]{:S(2)}) copy-start(pred[4]{0:T(512)(128)(4,1)} %get-tuple-element.123) | copy-start | bytes 16
  38.1 94.4 %copy-start.21 = (pred[256]{0:T(512)(128)(4,1)}, pred[256]{0:T(512)(128)(4,1)S(1)}, u32[]{:S(2)}) copy-start(pred[256]{0:T(512)(128)(4,1)S(1)} %get-tuple-element.120) | copy-start | bytes 772
  38.2 3.7 %collective-permute-start.18 = (f32[2,16,4,1]{3,1,2,0:T(8,128)S(1)}, f32[2,16,4,1]{3,1,2,0:T(8,128)S(1)}, u32[]{:S(2)}, u32[]{:S(2)}) collective-permute-start(f32[2,16,4,1]{3,1,2,0:T(8,128)S(1)} %get-tuple-element.91), channel_id=1, source_target_pairs={{0,1},{1,2},{2,3},{4,5},{5,6},{6,7},{8,9},{9,10},{10,11},{12,13},{... | collective-permute-start | bytes 1544 | tf_op jit(solution)/shard_map/ppermute | solution.py:21
  39.5 4.9 %collective-permute-start.19 = (f32[2,16,4,1]{3,1,2,0:T(8,128)S(1)}, f32[2,16,4,1]{3,1,2,0:T(8,128)S(1)}, u32[]{:S(2)}, u32[]{:S(2)}) collective-permute-start(f32[2,16,4,1]{3,1,2,0:T(8,128)S(1)} %get-tuple-element.92), channel_id=1, source_target_pairs={{1,0},{2,1},{3,2},{5,4},{6,5},{7,6},{9,8},{10,9},{11,10},{13,12},{... | collective-permute-start | bytes 1544 | tf_op jit(solution)/shard_map/ppermute | solution.py:23
  46.0 12.1 %collective-permute-start.20 = (f32[2,16,1,128]{3,1,2,0:T(8,128)S(1)}, f32[2,16,1,128]{3,1,2,0:T(8,128)S(1)}, u32[]{:S(2)}, u32[]{:S(2)}) collective-permute-start(f32[2,16,1,128]{3,1,2,0:T(8,128)S(1)} %get-tuple-element.105), channel_id=1, source_target_pairs={{0,4},{1,5},{2,6},{3,7},{8,12},{9,13},{10,14},{11,15},{16,20},{17,... | collective-permute-start | bytes 49160 | tf_op jit(solution)/shard_map/ppermute | solution.py:21
  50.5 7.6 %collective-permute-start.21 = (f32[2,16,1,128]{3,1,2,0:T(8,128)S(1)}, f32[2,16,1,128]{3,1,2,0:T(8,128)S(1)}, u32[]{:S(2)}, u32[]{:S(2)}) collective-permute-start(f32[2,16,1,128]{3,1,2,0:T(8,128)S(1)} %get-tuple-element.106), channel_id=1, source_target_pairs={{4,0},{5,1},{6,2},{7,3},{12,8},{13,9},{14,10},{15,11},{20,16},{21,... | collective-permute-start | bytes 49160 | tf_op jit(solution)/shard_map/ppermute | solution.py:23
  52.0 6.1 %collective-permute-start.2 = (f32[2,32,6,1]{3,1,2,0:T(8,128)S(1)}, f32[2,32,6,1]{3,1,2,0:T(8,128)S(1)}, u32[]{:S(2)}, u32[]{:S(2)}) collective-permute-start(f32[2,32,6,1]{3,1,2,0:T(8,128)S(1)} %get-tuple-element.49), channel_id=1, source_target_pairs={{0,1},{1,2},{2,3},{4,5},{5,6},{6,7},{8,9},{9,10},{10,11},{12,13},{... | collective-permute-start | bytes 4616 | tf_op jit(solution)/shard_map/ppermute | solution.py:21
  56.6 3.3 %collective-permute-start.3 = (f32[2,32,6,1]{3,1,2,0:T(8,128)S(1)}, f32[2,32,6,1]{3,1,2,0:T(8,128)S(1)}, u32[]{:S(2)}, u32[]{:S(2)}) collective-permute-start(f32[2,32,6,1]{3,1,2,0:T(8,128)S(1)} %get-tuple-element.50), channel_id=1, source_target_pairs={{1,0},{2,1},{3,2},{5,4},{6,5},{7,6},{9,8},{10,9},{11,10},{13,12},{... | collective-permute-start | bytes 4616 | tf_op jit(solution)/shard_map/ppermute | solution.py:23
  60.9 37.0 %copy-start.1 = (f32[4,256]{1,0:T(4,128)S(1)}, f32[4,256]{1,0:T(4,128)}, u32[]{:S(2)}) copy-start(f32[4,256]{1,0:T(4,128)} %get-tuple-element.116) | copy-start | bytes 12292
  60.9 37.0 %copy-start.23 = (pred[256]{0:T(512)(128)(4,1)S(1)}, pred[256]{0:T(512)(128)(4,1)}, u32[]{:S(2)}) copy-start(pred[256]{0:T(512)(128)(4,1)} %get-tuple-element.121) | copy-start | bytes 772
  74.7 13.4 %collective-permute-start.4 = (f32[2,32,1,256]{3,1,2,0:T(8,128)S(1)}, f32[2,32,1,256]{3,1,2,0:T(8,128)S(1)}, u32[]{:S(2)}, u32[]{:S(2)}) collective-permute-start(f32[2,32,1,256]{3,1,2,0:T(8,128)S(1)} %get-tuple-element.55), channel_id=1, source_target_pairs={{0,4},{1,5},{2,6},{3,7},{8,12},{9,13},{10,14},{11,15},{16,20},{17,... | collective-permute-start | bytes 196616 | tf_op jit(solution)/shard_map/ppermute | solution.py:21
  79.0 9.1 %collective-permute-start.5 = (f32[2,32,1,256]{3,1,2,0:T(8,128)S(1)}, f32[2,32,1,256]{3,1,2,0:T(8,128)S(1)}, u32[]{:S(2)}, u32[]{:S(2)}) collective-permute-start(f32[2,32,1,256]{3,1,2,0:T(8,128)S(1)} %get-tuple-element.56), channel_id=1, source_target_pairs={{4,0},{5,1},{6,2},{7,3},{12,8},{13,9},{14,10},{15,11},{20,16},{21,... | collective-permute-start | bytes 196616 | tf_op jit(solution)/shard_map/ppermute | solution.py:23
  81.0 36.2 %collective-permute-start.22 = (f32[2,16,4,1]{3,1,2,0:T(8,128)}, f32[2,16,4,1]{3,1,2,0:T(8,128)S(1)}, u32[]{:S(2)}, u32[]{:S(2)}) collective-permute-start(f32[2,16,4,1]{3,1,2,0:T(8,128)} %get-tuple-element.89), channel_id=1, source_target_pairs={{0,1},{1,2},{2,3},{4,5},{5,6},{6,7},{8,9},{9,10},{10,11},{12,13},{... | collective-permute-start | bytes 1544 | tf_op jit(solution)/shard_map/ppermute | solution.py:21
  86.8 30.4 %collective-permute-start.23 = (f32[2,16,4,1]{3,1,2,0:T(8,128)}, f32[2,16,4,1]{3,1,2,0:T(8,128)}, u32[]{:S(2)}, u32[]{:S(2)}) collective-permute-start(f32[2,16,4,1]{3,1,2,0:T(8,128)} %get-tuple-element.90), channel_id=1, source_target_pairs={{1,0},{2,1},{3,2},{5,4},{6,5},{7,6},{9,8},{10,9},{11,10},{13,12},{... | collective-permute-start | bytes 1544 | tf_op jit(solution)/shard_map/ppermute | solution.py:23
  88.3 8.7 %collective-permute-start.6 = (f32[2,32,6,1]{3,1,2,0:T(8,128)S(1)}, f32[2,32,6,1]{3,1,2,0:T(8,128)S(1)}, u32[]{:S(2)}, u32[]{:S(2)}) collective-permute-start(f32[2,32,6,1]{3,1,2,0:T(8,128)S(1)} %get-tuple-element.47), channel_id=1, source_target_pairs={{0,1},{1,2},{2,3},{4,5},{5,6},{6,7},{8,9},{9,10},{10,11},{12,13},{... | collective-permute-start | bytes 4616 | tf_op jit(solution)/shard_map/ppermute | solution.py:21
  91.3 5.7 %collective-permute-start.7 = (f32[2,32,6,1]{3,1,2,0:T(8,128)S(1)}, f32[2,32,6,1]{3,1,2,0:T(8,128)S(1)}, u32[]{:S(2)}, u32[]{:S(2)}) collective-permute-start(f32[2,32,6,1]{3,1,2,0:T(8,128)S(1)} %get-tuple-element.48), channel_id=1, source_target_pairs={{1,0},{2,1},{3,2},{5,4},{6,5},{7,6},{9,8},{10,9},{11,10},{13,12},{... | collective-permute-start | bytes 4616 | tf_op jit(solution)/shard_map/ppermute | solution.py:23
  111.7 6.6 %collective-permute-start.8 = (f32[2,32,1,256]{3,1,2,0:T(8,128)S(1)}, f32[2,32,1,256]{3,1,2,0:T(8,128)S(1)}, u32[]{:S(2)}, u32[]{:S(2)}) collective-permute-start(f32[2,32,1,256]{3,1,2,0:T(8,128)S(1)} %get-tuple-element.53), channel_id=1, source_target_pairs={{0,4},{1,5},{2,6},{3,7},{8,12},{9,13},{10,14},{11,15},{16,20},{17,... | collective-permute-start | bytes 196616 | tf_op jit(solution)/shard_map/ppermute | solution.py:21
  115.9 6.2 %collective-permute-start.9 = (f32[2,32,1,256]{3,1,2,0:T(8,128)S(1)}, f32[2,32,1,256]{3,1,2,0:T(8,128)S(1)}, u32[]{:S(2)}, u32[]{:S(2)}) collective-permute-start(f32[2,32,1,256]{3,1,2,0:T(8,128)S(1)} %get-tuple-element.54), channel_id=1, source_target_pairs={{4,0},{5,1},{6,2},{7,3},{12,8},{13,9},{14,10},{15,11},{20,16},{21,... | collective-permute-start | bytes 196616 | tf_op jit(solution)/shard_map/ppermute | solution.py:23
  122.2 9.4 %collective-permute-start.10 = (f32[2,32,6,1]{3,1,2,0:T(8,128)S(1)}, f32[2,32,6,1]{3,1,2,0:T(8,128)S(1)}, u32[]{:S(2)}, u32[]{:S(2)}) collective-permute-start(f32[2,32,6,1]{3,1,2,0:T(8,128)S(1)} %get-tuple-element.45), channel_id=1, source_target_pairs={{0,1},{1,2},{2,3},{4,5},{5,6},{6,7},{8,9},{9,10},{10,11},{12,13},{... | collective-permute-start | bytes 4616 | tf_op jit(solution)/shard_map/ppermute | solution.py:21
  125.7 5.9 %collective-permute-start.11 = (f32[2,32,6,1]{3,1,2,0:T(8,128)S(1)}, f32[2,32,6,1]{3,1,2,0:T(8,128)S(1)}, u32[]{:S(2)}, u32[]{:S(2)}) collective-permute-start(f32[2,32,6,1]{3,1,2,0:T(8,128)S(1)} %get-tuple-element.46), channel_id=1, source_target_pairs={{1,0},{2,1},{3,2},{5,4},{6,5},{7,6},{9,8},{10,9},{11,10},{13,12},{... | collective-permute-start | bytes 4616 | tf_op jit(solution)/shard_map/ppermute | solution.py:23
  146.3 3.8 %collective-permute-start.12 = (f32[2,32,1,256]{3,1,2,0:T(8,128)S(1)}, f32[2,32,1,256]{3,1,2,0:T(8,128)S(1)}, u32[]{:S(2)}, u32[]{:S(2)}) collective-permute-start(f32[2,32,1,256]{3,1,2,0:T(8,128)S(1)} %get-tuple-element.51), channel_id=1, source_target_pairs={{0,4},{1,5},{2,6},{3,7},{8,12},{9,13},{10,14},{11,15},{16,20},{17,... | collective-permute-start | bytes 196616 | tf_op jit(solution)/shard_map/ppermute | solution.py:21
  148.1 6.2 %collective-permute-start.13 = (f32[2,32,1,256]{3,1,2,0:T(8,128)S(1)}, f32[2,32,1,256]{3,1,2,0:T(8,128)S(1)}, u32[]{:S(2)}, u32[]{:S(2)}) collective-permute-start(f32[2,32,1,256]{3,1,2,0:T(8,128)S(1)} %get-tuple-element.52), channel_id=1, source_target_pairs={{4,0},{5,1},{6,2},{7,3},{12,8},{13,9},{14,10},{15,11},{20,16},{21,... | collective-permute-start | bytes 196616 | tf_op jit(solution)/shard_map/ppermute | solution.py:23
  154.4 9.4 %collective-permute-start.14 = (f32[2,32,6,1]{3,1,2,0:T(8,128)S(1)}, f32[2,32,6,1]{3,1,2,0:T(8,128)S(1)}, u32[]{:S(2)}, u32[]{:S(2)}) collective-permute-start(f32[2,32,6,1]{3,1,2,0:T(8,128)S(1)} %get-tuple-element.43), channel_id=1, source_target_pairs={{0,1},{1,2},{2,3},{4,5},{5,6},{6,7},{8,9},{9,10},{10,11},{12,13},{... | collective-permute-start | bytes 4616 | tf_op jit(solution)/shard_map/ppermute | solution.py:21
  158.2 5.7 %collective-permute-start.15 = (f32[2,32,6,1]{3,1,2,0:T(8,128)S(1)}, f32[2,32,6,1]{3,1,2,0:T(8,128)S(1)}, u32[]{:S(2)}, u32[]{:S(2)}) collective-permute-start(f32[2,32,6,1]{3,1,2,0:T(8,128)S(1)} %get-tuple-element.44), channel_id=1, source_target_pairs={{1,0},{2,1},{3,2},{5,4},{6,5},{7,6},{9,8},{10,9},{11,10},{13,12},{... | collective-permute-start | bytes 4616 | tf_op jit(solution)/shard_map/ppermute | solution.py:23
  186.2 5.6 %collective-permute-start.24 = (f32[16,2,128]{2,0,1:T(8,128)S(1)}, f32[16,2,128]{2,0,1:T(8,128)S(1)}, u32[]{:S(2)}, u32[]{:S(2)}) collective-permute-start(f32[16,2,128]{2,0,1:T(8,128)S(1)} %get-tuple-element.25), channel_id=1, source_target_pairs={{0,8},{8,16},{16,24},{1,9},{9,17},{17,25},{2,10},{10,18},{18,26},{... | collective-permute-start | bytes 49160 | tf_op jit(solution)/shard_map/ppermute | solution.py:33
  191.9 3.3 %collective-permute-start.25 = (f32[2,16,1,128]{3,1,2,0:T(8,128)S(1)}, f32[2,16,1,128]{3,1,2,0:T(8,128)S(1)}, u32[]{:S(2)}, u32[]{:S(2)}) collective-permute-start(f32[2,16,1,128]{3,1,2,0:T(8,128)S(1)} %get-tuple-element.103), channel_id=1, source_target_pairs={{0,4},{1,5},{2,6},{3,7},{8,12},{9,13},{10,14},{11,15},{16,20},{17,... | collective-permute-start | bytes 49160 | tf_op jit(solution)/shard_map/ppermute | solution.py:21
  193.8 5.6 %collective-permute-start.26 = (f32[2,16,1,128]{3,1,2,0:T(8,128)S(1)}, f32[2,16,1,128]{3,1,2,0:T(8,128)S(1)}, u32[]{:S(2)}, u32[]{:S(2)}) collective-permute-start(f32[2,16,1,128]{3,1,2,0:T(8,128)S(1)} %get-tuple-element.104), channel_id=1, source_target_pairs={{4,0},{5,1},{6,2},{7,3},{12,8},{13,9},{14,10},{15,11},{20,16},{21,... | collective-permute-start | bytes 49160 | tf_op jit(solution)/shard_map/ppermute | solution.py:23
  199.5 4.4 %collective-permute-start.27 = (f32[2,16,4,1]{3,1,2,0:T(8,128)S(1)}, f32[2,16,4,1]{3,1,2,0:T(8,128)S(1)}, u32[]{:S(2)}, u32[]{:S(2)}) collective-permute-start(f32[2,16,4,1]{3,1,2,0:T(8,128)S(1)} %get-tuple-element.87), channel_id=1, source_target_pairs={{0,1},{1,2},{2,3},{4,5},{5,6},{6,7},{8,9},{9,10},{10,11},{12,13},{... | collective-permute-start | bytes 1544 | tf_op jit(solution)/shard_map/ppermute | solution.py:21
  202.6 6.3 %collective-permute-start.28 = (f32[2,16,4,1]{3,1,2,0:T(8,128)S(1)}, f32[2,16,4,1]{3,1,2,0:T(8,128)S(1)}, u32[]{:S(2)}, u32[]{:S(2)}) collective-permute-start(f32[2,16,4,1]{3,1,2,0:T(8,128)S(1)} %get-tuple-element.88), channel_id=1, source_target_pairs={{1,0},{2,1},{3,2},{5,4},{6,5},{7,6},{9,8},{10,9},{11,10},{13,12},{... | collective-permute-start | bytes 1544 | tf_op jit(solution)/shard_map/ppermute | solution.py:23
  209.3 3.1 %collective-permute-start.29 = (f32[2,16,1,128]{3,1,2,0:T(8,128)S(1)}, f32[2,16,1,128]{3,1,2,0:T(8,128)S(1)}, u32[]{:S(2)}, u32[]{:S(2)}) collective-permute-start(f32[2,16,1,128]{3,1,2,0:T(8,128)S(1)} %get-tuple-element.101), channel_id=1, source_target_pairs={{0,4},{1,5},{2,6},{3,7},{8,12},{9,13},{10,14},{11,15},{16,20},{17,... | collective-permute-start | bytes 49160 | tf_op jit(solution)/shard_map/ppermute | solution.py:21
  210.9 5.6 %collective-permute-start.30 = (f32[2,16,1,128]{3,1,2,0:T(8,128)S(1)}, f32[2,16,1,128]{3,1,2,0:T(8,128)S(1)}, u32[]{:S(2)}, u32[]{:S(2)}) collective-permute-start(f32[2,16,1,128]{3,1,2,0:T(8,128)S(1)} %get-tuple-element.102), channel_id=1, source_target_pairs={{4,0},{5,1},{6,2},{7,3},{12,8},{13,9},{14,10},{15,11},{20,16},{21,... | collective-permute-start | bytes 49160 | tf_op jit(solution)/shard_map/ppermute | solution.py:23
  216.6 4.8 %collective-permute-start.31 = (f32[2,16,4,1]{3,1,2,0:T(8,128)S(1)}, f32[2,16,4,1]{3,1,2,0:T(8,128)S(1)}, u32[]{:S(2)}, u32[]{:S(2)}) collective-permute-start(f32[2,16,4,1]{3,1,2,0:T(8,128)S(1)} %get-tuple-element.85), channel_id=1, source_target_pairs={{0,1},{1,2},{2,3},{4,5},{5,6},{6,7},{8,9},{9,10},{10,11},{12,13},{... | collective-permute-start | bytes 1544 | tf_op jit(solution)/shard_map/ppermute | solution.py:21
  220.0 4.0 %collective-permute-start.32 = (f32[2,16,4,1]{3,1,2,0:T(8,128)S(1)}, f32[2,16,4,1]{3,1,2,0:T(8,128)S(1)}, u32[]{:S(2)}, u32[]{:S(2)}) collective-permute-start(f32[2,16,4,1]{3,1,2,0:T(8,128)S(1)} %get-tuple-element.86), channel_id=1, source_target_pairs={{1,0},{2,1},{3,2},{5,4},{6,5},{7,6},{9,8},{10,9},{11,10},{13,12},{... | collective-permute-start | bytes 1544 | tf_op jit(solution)/shard_map/ppermute | solution.py:23
  224.4 5.6 %collective-permute-start.33 = (f32[16,2,128]{2,0,1:T(8,128)S(1)}, f32[16,2,128]{2,0,1:T(8,128)S(1)}, u32[]{:S(2)}, u32[]{:S(2)}) collective-permute-start(f32[16,2,128]{2,0,1:T(8,128)S(1)} %fusion.173), channel_id=1, source_target_pairs={{0,8},{8,16},{16,24},{1,9},{9,17},{17,25},{2,10},{10,18},{18,26},{... | collective-permute-start | bytes 49160 | tf_op jit(solution)/shard_map/ppermute | solution.py:33
  230.1 3.1 %collective-permute-start.34 = (f32[2,16,1,128]{3,1,2,0:T(8,128)S(1)}, f32[2,16,1,128]{3,1,2,0:T(8,128)S(1)}, u32[]{:S(2)}, u32[]{:S(2)}) collective-permute-start(f32[2,16,1,128]{3,1,2,0:T(8,128)S(1)} %get-tuple-element.99), channel_id=1, source_target_pairs={{0,4},{1,5},{2,6},{3,7},{8,12},{9,13},{10,14},{11,15},{16,20},{17,... | collective-permute-start | bytes 49160 | tf_op jit(solution)/shard_map/ppermute | solution.py:21
  231.8 5.6 %collective-permute-start.35 = (f32[2,16,1,128]{3,1,2,0:T(8,128)S(1)}, f32[2,16,1,128]{3,1,2,0:T(8,128)S(1)}, u32[]{:S(2)}, u32[]{:S(2)}) collective-permute-start(f32[2,16,1,128]{3,1,2,0:T(8,128)S(1)} %get-tuple-element.100), channel_id=1, source_target_pairs={{4,0},{5,1},{6,2},{7,3},{12,8},{13,9},{14,10},{15,11},{20,16},{21,... | collective-permute-start | bytes 49160 | tf_op jit(solution)/shard_map/ppermute | solution.py:23
  237.5 3.6 %collective-permute-start.36 = (f32[2,16,4,1]{3,1,2,0:T(8,128)S(1)}, f32[2,16,4,1]{3,1,2,0:T(8,128)S(1)}, u32[]{:S(2)}, u32[]{:S(2)}) collective-permute-start(f32[2,16,4,1]{3,1,2,0:T(8,128)S(1)} %get-tuple-element.83), channel_id=1, source_target_pairs={{0,1},{1,2},{2,3},{4,5},{5,6},{6,7},{8,9},{9,10},{10,11},{12,13},{... | collective-permute-start | bytes 1544 | tf_op jit(solution)/shard_map/ppermute | solution.py:21
  239.7 5.2 %collective-permute-start.37 = (f32[2,16,4,1]{3,1,2,0:T(8,128)S(1)}, f32[2,16,4,1]{3,1,2,0:T(8,128)S(1)}, u32[]{:S(2)}, u32[]{:S(2)}) collective-permute-start(f32[2,16,4,1]{3,1,2,0:T(8,128)S(1)} %get-tuple-element.84), channel_id=1, source_target_pairs={{1,0},{2,1},{3,2},{5,4},{6,5},{7,6},{9,8},{10,9},{11,10},{13,12},{... | collective-permute-start | bytes 1544 | tf_op jit(solution)/shard_map/ppermute | solution.py:23
  245.3 3.1 %collective-permute-start.38 = (f32[2,16,1,128]{3,1,2,0:T(8,128)S(1)}, f32[2,16,1,128]{3,1,2,0:T(8,128)S(1)}, u32[]{:S(2)}, u32[]{:S(2)}) collective-permute-start(f32[2,16,1,128]{3,1,2,0:T(8,128)S(1)} %get-tuple-element.97), channel_id=1, source_target_pairs={{0,4},{1,5},{2,6},{3,7},{8,12},{9,13},{10,14},{11,15},{16,20},{17,... | collective-permute-start | bytes 49160 | tf_op jit(solution)/shard_map/ppermute | solution.py:21
  246.9 5.6 %collective-permute-start.39 = (f32[2,16,1,128]{3,1,2,0:T(8,128)S(1)}, f32[2,16,1,128]{3,1,2,0:T(8,128)S(1)}, u32[]{:S(2)}, u32[]{:S(2)}) collective-permute-start(f32[2,16,1,128]{3,1,2,0:T(8,128)S(1)} %get-tuple-element.98), channel_id=1, source_target_pairs={{4,0},{5,1},{6,2},{7,3},{12,8},{13,9},{14,10},{15,11},{20,16},{21,... | collective-permute-start | bytes 49160 | tf_op jit(solution)/shard_map/ppermute | solution.py:23
  252.7 4.8 %collective-permute-start.40 = (f32[2,16,4,1]{3,1,2,0:T(8,128)S(1)}, f32[2,16,4,1]{3,1,2,0:T(8,128)S(1)}, u32[]{:S(2)}, u32[]{:S(2)}) collective-permute-start(f32[2,16,4,1]{3,1,2,0:T(8,128)S(1)} %get-tuple-element.81), channel_id=1, source_target_pairs={{0,1},{1,2},{2,3},{4,5},{5,6},{6,7},{8,9},{9,10},{10,11},{12,13},{... | collective-permute-start | bytes 1544 | tf_op jit(solution)/shard_map/ppermute | solution.py:21
  256.1 4.0 %collective-permute-start.41 = (f32[2,16,4,1]{3,1,2,0:T(8,128)S(1)}, f32[2,16,4,1]{3,1,2,0:T(8,128)S(1)}, u32[]{:S(2)}, u32[]{:S(2)}) collective-permute-start(f32[2,16,4,1]{3,1,2,0:T(8,128)S(1)} %get-tuple-element.82), channel_id=1, source_target_pairs={{1,0},{2,1},{3,2},{5,4},{6,5},{7,6},{9,8},{10,9},{11,10},{13,12},{... | collective-permute-start | bytes 1544 | tf_op jit(solution)/shard_map/ppermute | solution.py:23
  260.4 5.6 %collective-permute-start.42 = (f32[16,2,128]{2,0,1:T(8,128)S(1)}, f32[16,2,128]{2,0,1:T(8,128)S(1)}, u32[]{:S(2)}, u32[]{:S(2)}) collective-permute-start(f32[16,2,128]{2,0,1:T(8,128)S(1)} %fusion.194), channel_id=1, source_target_pairs={{0,8},{8,16},{16,24},{1,9},{9,17},{17,25},{2,10},{10,18},{18,26},{... | collective-permute-start | bytes 49160 | tf_op jit(solution)/shard_map/ppermute | solution.py:33
  266.1 3.1 %collective-permute-start.43 = (f32[2,16,1,128]{3,1,2,0:T(8,128)S(1)}, f32[2,16,1,128]{3,1,2,0:T(8,128)S(1)}, u32[]{:S(2)}, u32[]{:S(2)}) collective-permute-start(f32[2,16,1,128]{3,1,2,0:T(8,128)S(1)} %get-tuple-element.95), channel_id=1, source_target_pairs={{0,4},{1,5},{2,6},{3,7},{8,12},{9,13},{10,14},{11,15},{16,20},{17,... | collective-permute-start | bytes 49160 | tf_op jit(solution)/shard_map/ppermute | solution.py:21
  267.8 5.6 %collective-permute-start.44 = (f32[2,16,1,128]{3,1,2,0:T(8,128)S(1)}, f32[2,16,1,128]{3,1,2,0:T(8,128)S(1)}, u32[]{:S(2)}, u32[]{:S(2)}) collective-permute-start(f32[2,16,1,128]{3,1,2,0:T(8,128)S(1)} %get-tuple-element.96), channel_id=1, source_target_pairs={{4,0},{5,1},{6,2},{7,3},{12,8},{13,9},{14,10},{15,11},{20,16},{21,... | collective-permute-start | bytes 49160 | tf_op jit(solution)/shard_map/ppermute | solution.py:23
  273.5 3.6 %collective-permute-start.45 = (f32[2,16,4,1]{3,1,2,0:T(8,128)S(1)}, f32[2,16,4,1]{3,1,2,0:T(8,128)S(1)}, u32[]{:S(2)}, u32[]{:S(2)}) collective-permute-start(f32[2,16,4,1]{3,1,2,0:T(8,128)S(1)} %get-tuple-element.79), channel_id=1, source_target_pairs={{0,1},{1,2},{2,3},{4,5},{5,6},{6,7},{8,9},{9,10},{10,11},{12,13},{... | collective-permute-start | bytes 1544 | tf_op jit(solution)/shard_map/ppermute | solution.py:21
  275.8 5.2 %collective-permute-start.46 = (f32[2,16,4,1]{3,1,2,0:T(8,128)S(1)}, f32[2,16,4,1]{3,1,2,0:T(8,128)S(1)}, u32[]{:S(2)}, u32[]{:S(2)}) collective-permute-start(f32[2,16,4,1]{3,1,2,0:T(8,128)S(1)} %get-tuple-element.80), channel_id=1, source_target_pairs={{1,0},{2,1},{3,2},{5,4},{6,5},{7,6},{9,8},{10,9},{11,10},{13,12},{... | collective-permute-start | bytes 1544 | tf_op jit(solution)/shard_map/ppermute | solution.py:23
  281.3 3.1 %collective-permute-start.47 = (f32[2,16,1,128]{3,1,2,0:T(8,128)S(1)}, f32[2,16,1,128]{3,1,2,0:T(8,128)S(1)}, u32[]{:S(2)}, u32[]{:S(2)}) collective-permute-start(f32[2,16,1,128]{3,1,2,0:T(8,128)S(1)} %get-tuple-element.93), channel_id=1, source_target_pairs={{0,4},{1,5},{2,6},{3,7},{8,12},{9,13},{10,14},{11,15},{16,20},{17,... | collective-permute-start | bytes 49160 | tf_op jit(solution)/shard_map/ppermute | solution.py:21
  283.0 5.6 %collective-permute-start.48 = (f32[2,16,1,128]{3,1,2,0:T(8,128)S(1)}, f32[2,16,1,128]{3,1,2,0:T(8,128)S(1)}, u32[]{:S(2)}, u32[]{:S(2)}) collective-permute-start(f32[2,16,1,128]{3,1,2,0:T(8,128)S(1)} %get-tuple-element.94), channel_id=1, source_target_pairs={{4,0},{5,1},{6,2},{7,3},{12,8},{13,9},{14,10},{15,11},{20,16},{21,... | collective-permute-start | bytes 49160 | tf_op jit(solution)/shard_map/ppermute | solution.py:23
  288.7 4.8 %collective-permute-start.49 = (f32[2,16,4,1]{3,1,2,0:T(8,128)S(1)}, f32[2,16,4,1]{3,1,2,0:T(8,128)S(1)}, u32[]{:S(2)}, u32[]{:S(2)}) collective-permute-start(f32[2,16,4,1]{3,1,2,0:T(8,128)S(1)} %get-tuple-element.77), channel_id=1, source_target_pairs={{0,1},{1,2},{2,3},{4,5},{5,6},{6,7},{8,9},{9,10},{10,11},{12,13},{... | collective-permute-start | bytes 1544 | tf_op jit(solution)/shard_map/ppermute | solution.py:21
  292.1 4.0 %collective-permute-start.50 = (f32[2,16,4,1]{3,1,2,0:T(8,128)S(1)}, f32[2,16,4,1]{3,1,2,0:T(8,128)S(1)}, u32[]{:S(2)}, u32[]{:S(2)}) collective-permute-start(f32[2,16,4,1]{3,1,2,0:T(8,128)S(1)} %get-tuple-element.78), channel_id=1, source_target_pairs={{1,0},{2,1},{3,2},{5,4},{6,5},{7,6},{9,8},{10,9},{11,10},{13,12},{... | collective-permute-start | bytes 1544 | tf_op jit(solution)/shard_map/ppermute | solution.py:23
  (15 other events, 200.9 us)
where the time goes:
time: 303 us; the launch traced here: 298 us
  starting transfers between devices  115 us (38%)
  other arithmetic  80.4 us (27%)
  waiting for transfers between devices  66 us (22%)
  local copies, waits for them, and re-layouts  35 us (12%)
    ppermute x24, starting transfers between devices, with_halo(): lax.ppermute(tail, axis, [(i, (i + 1) % count) for i in range(ends)])  72.5 us
    ppermute x24, waiting for transfers between devices, with_halo(): lax.ppermute(head, axis, [((i + 1) % count, i) for i in range(ends)])  58.5 us
    mul x12, other arithmetic, conductivity(): saturated * jnp.sqrt(jnp.power(1.0 + powered, -exponent))  35 us
    ppermute x24, starting transfers between devices, with_halo(): lax.ppermute(head, axis, [((i + 1) % count, i) for i in range(ends)])  31.4 us
    ppermute x3, starting transfers between devices, from_behind(): return lax.ppermute(array, axis, pairs)  10.7 us
    another operation x1, local copies, waits for them, and re-layouts, restrict(): field.reshape(depth // 2, 2, rows // 2, 2, columns // 2, 2)  9.82 us
    reshape x1, local copies, waits for them, and re-layouts, restrict(): field.reshape(depth // 2, 2, rows // 2, 2, columns // 2, 2)  9.82 us
    another operation x11, other arithmetic, run_steps(): stacked = jnp.stack([heads, conduct])  9.67 us
  transfers between devices with their start and end apart: 51, of which 26 were waited for; matrix products, arithmetic and copies ran while one was open for 19% of the time, Pallas kernels for 0%

commit v1 on v0

--- a/solution.py
+++ b/solution.py
@@ -1,6 +1,10 @@
+import functools
+
 import jax
 import jax.numpy as jnp
 from jax import lax
+from jax.experimental import pallas as pl
+from jax.experimental.pallas import tpu as pltpu
 from jax.sharding import PartitionSpec as P
 
 FINE_STEPS = 4
@@ -188,6 +192,513 @@
     return end_state[None]
 
 
+MESH = pl.DeviceIdType.MESH
+EXTRA = 128
+
+
+def closure(heads, entry, power, half_exponent, half_saturated, gain, interval):
+    suction = jnp.maximum(-heads, 0.0) * entry
+    lifted = jnp.exp(power * jnp.log(jnp.maximum(suction, 1e-37)))
+    grown = 1.0 + suction * lifted
+    root = jnp.exp(half_exponent * jnp.log(grown))
+    wetted = lifted * root * root
+    dry = 1.0 - wetted
+    half_conduct = half_saturated * root * dry * dry
+    rate = interval * grown / (STORAGE * grown + gain * wetted)
+    return half_conduct, rate
+
+
+def derived(saturated, entry, shape_index, porosity):
+    power = shape_index - 1.0
+    return (
+        entry,
+        power,
+        -0.5 * power / shape_index,
+        0.5 * saturated,
+        porosity * power * entry,
+    )
+
+
+def shifted(array, by, axis):
+    return pltpu.roll(array, by % array.shape[axis], axis)
+
+
+def vertical(heads, half, source, spacing):
+    depth = heads.shape[0]
+    place = lax.broadcasted_iota(jnp.int32, heads.shape, 0)
+    below = shifted(heads, -1, 0)
+    flow = (half + shifted(half, -1, 0)) * ((heads - below) * (1.0 / spacing) + 1.0)
+    outflow = jnp.where(place == depth - 1, 2.0 * half, flow)
+    inflow = jnp.where(place == 0, source, shifted(outflow, 1, 0))
+    return (inflow - outflow) * (1.0 / spacing)
+
+
+def coarse_steps(own, other, params, steps, column_open, even):
+    wide = 2.0
+    pairs = [own, other]
+    for s in range(steps):
+        closed = [
+            closure(pairs[w], *params[w][:5], wide) for w in range(2)
+        ]
+        across = jnp.where(
+            even, 0.0, (closed[0][0] + closed[1][0]) * (pairs[1] - pairs[0])
+        )
+        fresh = []
+        for w in range(2):
+            if w == 1 and s == steps - 1:
+                fresh.append(pairs[1])
+                continue
+            heads, (half, rate) = pairs[w], closed[w]
+            right = column_open * (half + shifted(half, -2, 1)) * (shifted(heads, -2, 1) - heads)
+            lateral = right - shifted(right, 2, 1)
+            twin = jnp.where(even, shifted(heads, -1, 1), shifted(heads, 1, 1))
+            twin_half = jnp.where(even, shifted(half, -1, 1), shifted(half, 1, 1))
+            lateral = lateral + (half + twin_half) * (twin - heads)
+            lateral = lateral + across if w == 0 else lateral - across
+            balance = lateral * (1.0 / (wide * wide)) + vertical(heads, half, params[w][5], wide)
+            fresh.append(heads + rate * balance)
+        pairs = fresh
+    return pairs[0]
+
+
+def pair_kernel(
+    sizes,
+    width,
+    heads_ref,
+    class_ref,
+    saturated_ref,
+    entry_ref,
+    shape_ref,
+    porosity_ref,
+    cell_ref,
+    plan_ref,
+    rates_ref,
+    out_ref,
+    field,
+    halves,
+    speeds,
+    table,
+    coarse_table,
+    aux_out,
+    aux_in,
+    edge_out,
+    edge_in,
+    fold,
+    old,
+    fresh,
+    correction,
+    chain_out,
+    chain_in,
+    row_send,
+    row_recv,
+    aux_send,
+    aux_recv,
+    edge_send,
+    edge_recv,
+    chain_send,
+    chain_recv,
+):
+    slices, column_tiles = sizes["cuts"], sizes["gy"]
+    _, depth, rows, columns = heads_ref.shape
+    span = columns + EXTRA
+    k = lax.axis_index("cuts")
+    gx = lax.axis_index("gx")
+    gy = lax.axis_index("gy")
+    low = gx == 0
+    has_left, has_right = gy > 0, gy < column_tiles - 1
+    has_before, has_after = k > 0, k < slices - 1
+    pieces = 128 // width
+
+    partner = (k, 1 - gx, gy)
+    greeted = (
+        (None, partner),
+        (has_left, (k, gx, gy - 1)),
+        (has_left, (k, 1 - gx, gy - 1)),
+        (has_right, (k, gx, gy + 1)),
+        (has_right, (k, 1 - gx, gy + 1)),
+        (has_before, (k - 1, gx, gy)),
+        (has_before, (k - 1, 1 - gx, gy)),
+        (has_after, (k + 1, gx, gy)),
+        (has_after, (k + 1, 1 - gx, gy)),
+    )
+    barrier = pltpu.get_barrier_semaphore()
+    for there, device in greeted:
+        def greet(device=device):
+            pl.semaphore_signal(barrier, inc=1, device_id=device, device_id_type=MESH)
+
+        if there is None:
+            greet()
+        else:
+            pl.when(there)(greet)
+
+    own = [heads_ref[0, :, r, :] for r in range(rows)]
+    for j in range(rows):
+        field[0, j, :, pl.ds(0, columns)] = jnp.where(low, own[j], own[rows - 1 - j])
+    classes = class_ref[...].astype(jnp.float32)
+    for j in range(rows):
+        aux_out[pl.ds(j, 1), :] = jnp.where(
+            low, classes[j : j + 1], classes[rows - 1 - j : rows - j]
+        )
+
+    kinds = rates_ref.shape[0]
+    picked = lax.broadcasted_iota(jnp.int32, rates_ref.shape, 1) == k
+    rate_of = jnp.sum(jnp.where(picked, rates_ref[...], 0.0), axis=1, keepdims=True)
+    plan = plan_ref[...]
+    cell = cell_ref[...]
+    count = plan.shape[1]
+    planned = plan == lax.broadcasted_iota(jnp.int32, (kinds, count), 0)
+    rates = jnp.sum(jnp.where(planned, rate_of, 0.0), axis=0, keepdims=True)
+    row_of, column_of = cell // columns, cell % columns
+    line = lax.broadcasted_iota(jnp.int32, (8, count), 0)
+    line = jnp.where(low, line, rows - 1 - line)
+    by_row = jnp.where(row_of == line, rates, 0.0)
+    by_column = jnp.where(
+        column_of == lax.broadcasted_iota(jnp.int32, (columns, count), 0), 1.0, 0.0
+    )
+    source = lax.dot_general(
+        by_row,
+        by_column,
+        (((1,), (1,)), ((), ())),
+        precision=lax.Precision.HIGHEST,
+        preferred_element_type=jnp.float32,
+    )
+    aux_out[pl.ds(rows, rows), :] = source[:rows]
+
+    lane = lax.broadcasted_iota(jnp.int32, (width, EXTRA), 1)
+    packs = [jnp.zeros((width, EXTRA), jnp.float32) for _ in range(2)]
+    per_row = depth // width
+    for p in range(pieces):
+        j, part = p // per_row, p % per_row
+        here = (lane >= p * width) & (lane < (p + 1) * width)
+        for side in range(2):
+            block = field[0, j, pl.ds(part * width, width), pl.ds(side * (columns - 128), 128)]
+            packs[side] = jnp.where(here, shifted(block, (p + side) * width, 1), packs[side])
+    for side in range(2):
+        edge_out[side, pl.ds(0, width), :] = packs[side]
+        edge_out[side, pl.ds(width, 8), :] = aux_out[:, pl.ds(side * (columns - 128), 128)]
+
+    def fill(side):
+        for who in range(2):
+            edge_in[side, who] = edge_out[side]
+
+    pl.when(jnp.logical_not(has_right))(lambda: fill(0))
+    pl.when(jnp.logical_not(has_left))(lambda: fill(1))
+
+    sides = [has_left, has_right, has_before, has_after]
+    pl.semaphore_wait(barrier, 1 + 2 * sum(there.astype(jnp.int32) for there in sides))
+
+    def copy(source_ref, target_ref, send, recv, device):
+        return pltpu.make_async_remote_copy(
+            src_ref=source_ref,
+            dst_ref=target_ref,
+            send_sem=send,
+            recv_sem=recv,
+            device_id=device,
+            device_id_type=MESH,
+        )
+
+    row_copies = [
+        copy(
+            field.at[0, j, :, pl.ds(0, columns)],
+            field.at[0, 2 * rows - 1 - j, :, pl.ds(0, columns)],
+            row_send.at[j],
+            row_recv.at[j],
+            partner,
+        )
+        for j in range(rows)
+    ]
+    aux_copy = copy(aux_out, aux_in, aux_send, aux_recv, partner)
+    edge_copies = [
+        [
+            copy(
+                edge_out.at[side],
+                edge_in.at[side, who],
+                edge_send.at[side, who],
+                edge_recv.at[side, who],
+                (k, gx if who == 0 else 1 - gx, gy - 1 if side == 0 else gy + 1),
+            )
+            for who in range(2)
+        ]
+        for side in range(2)
+    ]
+    sends_to = (has_left, has_right)
+    hears_from = (has_right, has_left)
+    for side in range(2):
+        @pl.when(sends_to[side])
+        def _():
+            for who in range(2):
+                edge_copies[side][who].start()
+    aux_copy.start()
+    for j in reversed(range(rows)):
+        row_copies[j].start()
+
+    for side in range(2):
+        @pl.when(hears_from[side])
+        def _():
+            for who in range(2):
+                edge_copies[side][who].wait_recv()
+    aux_copy.wait_recv()
+
+    third = lax.broadcasted_iota(jnp.int32, (width, EXTRA), 1)
+    for who in range(2):
+        for p in range(pieces):
+            j, part = p // per_row, p % per_row
+            from_right = shifted(edge_in[0, who, pl.ds(0, width), :], -p * width, 1)
+            from_left = shifted(edge_in[1, who, pl.ds(0, width), :], -(p + 1) * width, 1)
+            block = jnp.where(
+                third < width, from_right, jnp.where(third >= EXTRA - width, from_left, -1.0)
+            )
+            row = j if who == 0 else 2 * rows - 1 - j
+            field[0, row, pl.ds(part * width, width), pl.ds(columns, EXTRA)] = block
+
+    third8 = lax.broadcasted_iota(jnp.int32, (8, EXTRA), 1)
+    wide_aux = [
+        jnp.concatenate(
+            [
+                (aux_out if who == 0 else aux_in)[...],
+                jnp.where(
+                    third8 < EXTRA // 2,
+                    edge_in[0, who, pl.ds(width, 8), :],
+                    edge_in[1, who, pl.ds(width, 8), :],
+                ),
+            ],
+            axis=1,
+        )
+        for who in range(2)
+    ]
+    lanes = lax.broadcasted_iota(jnp.int32, (1, span), 1)
+    even = lanes % 2 == 0
+    column = gy * columns + jnp.where(lanes < columns + EXTRA // 2, lanes, lanes - span)
+    total = column_tiles * columns
+    fine_open = jnp.where((column >= 0) & (column + 1 < total), 1.0, 0.0)
+    coarse_open = jnp.where((column >= 0) & (column + 2 < total), 1.0, 0.0)
+
+    def paired(first, second):
+        return jnp.where(even, first + shifted(first, -1, 1), second + shifted(second, 1, 1))
+
+    refs = (saturated_ref, entry_ref, shape_ref, porosity_ref)
+    for who in range(2):
+        cls = wide_aux[who]
+        found = [jnp.zeros_like(cls) for _ in refs]
+        for c in range(saturated_ref.shape[0]):
+            match = cls == float(c)
+            found = [jnp.where(match, ref[c], f) for ref, f in zip(refs, found)]
+        src = wide_aux[who]
+        means = [
+            0.25 * paired(f[0:1] + f[1:2], f[2:3] + f[3:4]) for f in found
+        ]
+        spread = 0.25 * paired(
+            src[rows : rows + 1] + src[rows + 1 : rows + 2],
+            src[rows + 2 : rows + 3] + src[rows + 3 : rows + 4],
+        )
+        for i, value in enumerate(derived(*means) + (spread,)):
+            coarse_table[who, pl.ds(i, 1), :] = value
+        for i, value in enumerate(derived(*[f[:rows] for f in found]) + (src[rows:],)):
+            for j in range(rows):
+                row = j if who == 0 else 2 * rows - 1 - j
+                table[row, pl.ds(i, 1), :] = value[j : j + 1]
+
+    def coarse_params(who):
+        return [coarse_table[who, pl.ds(i, 1), :] for i in range(6)]
+
+    def restricted(slot, row_ids):
+        for q in range(2):
+            total = field[slot, row_ids[2 * q]] + field[slot, row_ids[2 * q + 1]]
+            for c in range(span // 128):
+                fold[q, c] = total[:, c * 128 : (c + 1) * 128]
+        sums = []
+        for q in range(2):
+            lines = [
+                fold[q, c, pl.ds(0, depth // 2, stride=2), :]
+                + fold[q, c, pl.ds(1, depth // 2, stride=2), :]
+                for c in range(span // 128)
+            ]
+            sums.append(jnp.concatenate(lines, axis=1))
+        return 0.125 * paired(*sums)
+
+    for j in reversed(range(rows)):
+        row_copies[j].wait_recv()
+
+    last = 2 * rows - 1
+    old[...] = coarse_steps(
+        restricted(0, (0, 1, 2, 3)),
+        restricted(0, (last, last - 1, last - 2, last - 3)),
+        [coarse_params(0), coarse_params(1)],
+        COARSE_STEPS,
+        coarse_open,
+        even,
+    )
+
+    for j in range(rows):
+        row_copies[j].wait_send()
+
+    for s in range(FINE_STEPS):
+        now, later = s % 2, (s + 1) % 2
+        reach = 2 * rows - 1 - s
+
+        def close(j, carry):
+            given = [table[j, pl.ds(i, 1), :] for i in range(5)]
+            half, rate = closure(field[now, j], *given, 1.0)
+            halves[j] = half
+            speeds[j] = rate
+            return carry
+
+        lax.fori_loop(0, reach + 1, close, 0)
+
+        def move(j, carry):
+            heads, half = field[now, j], halves[j]
+            right = fine_open * (half + shifted(half, -1, 1)) * (shifted(heads, -1, 1) - heads)
+            up = (half + halves[j + 1]) * (field[now, j + 1] - heads)
+            before = jnp.maximum(j - 1, 0)
+            down = (half + halves[before]) * (field[now, before] - heads)
+            balance = (
+                right
+                - shifted(right, 1, 1)
+                + up
+                + down
+                + vertical(heads, half, table[j, pl.ds(5, 1), :], 1.0)
+            )
+            field[later, j] = heads + speeds[j] * balance
+            return carry
+
+        lax.fori_loop(0, reach, move, 0)
+
+    done = FINE_STEPS % 2
+    correction[...] = restricted(done, (0, 1, 2, 3)) - old[...]
+
+    chain_copies = [
+        copy(
+            chain_out,
+            chain_in.at[who],
+            chain_send.at[who],
+            chain_recv.at[who],
+            (k + 1, gx if who == 0 else 1 - gx, gy),
+        )
+        for who in range(2)
+    ]
+
+    @pl.when(jnp.logical_not(has_before))
+    def _():
+        fresh[...] = old[...]
+
+    @pl.when(has_before)
+    def _():
+        for who in range(2):
+            chain_copies[who].wait_recv()
+        fresh[...] = coarse_steps(
+            chain_in[0],
+            chain_in[1],
+            [coarse_params(0), coarse_params(1)],
+            COARSE_STEPS,
+            coarse_open,
+            even,
+        )
+
+    @pl.when(has_after)
+    def _():
+        chain_out[...] = fresh[...] + correction[...]
+        for who in range(2):
+            chain_copies[who].start()
+
+    change = fresh[...] - old[...]
+    spread_rows = (
+        jnp.where(even, change, shifted(change, 1, 1)),
+        jnp.where(even, shifted(change, -1, 1), change),
+    )
+    for q in range(2):
+        for half in range(2):
+            for c in range(columns // 128):
+                fold[q, c, pl.ds(half, depth // 2, stride=2), :] = spread_rows[q][
+                    :, c * 128 : (c + 1) * 128
+                ]
+    ends = [
+        field[done, j, :, pl.ds(0, columns)]
+        + jnp.concatenate([fold[j // 2, c] for c in range(columns // 128)], axis=1)
+        for j in range(rows)
+    ]
+    for j in range(rows):
+        out_ref[j] = jnp.where(low, ends[j], ends[rows - 1 - j])
+
+    aux_copy.wait_send()
+    for side in range(2):
+        @pl.when(sends_to[side])
+        def _():
+            for who in range(2):
+                edge_copies[side][who].wait_send()
+
+    @pl.when(has_after)
+    def _():
+        for who in range(2):
+            chain_copies[who].wait_send()
+
+
+def on_pair(
+    sizes,
+    start_heads,
+    soil_class,
+    soil_conductivity,
+    soil_entry,
+    soil_shape,
+    soil_porosity,
+    emitter_cell,
+    emitter_plan,
+    plan_rates,
+):
+    _, depth, rows, columns = start_heads.shape
+    span = columns + EXTRA
+    width = 4 * sizes["cuts"]
+    vmem = pl.BlockSpec(memory_space=pltpu.VMEM)
+    smem = pl.BlockSpec(memory_space=pltpu.SMEM)
+    dma = pltpu.SemaphoreType.DMA
+    f32 = jnp.float32
+    half = (depth // 2, span)
+    ends = pl.pallas_call(
+        functools.partial(pair_kernel, dict(sizes), width),
+        out_shape=jax.ShapeDtypeStruct((rows, depth, columns), f32),
+        in_specs=[vmem, vmem, smem, smem, smem, smem, vmem, vmem, vmem],
+        out_specs=vmem,
+        scratch_shapes=[
+            pltpu.VMEM((2, 2 * rows, depth, span), f32),
+            pltpu.VMEM((2 * rows, depth, span), f32),
+            pltpu.VMEM((2 * rows, depth, span), f32),
+            pltpu.VMEM((2 * rows, 8, span), f32),
+            pltpu.VMEM((2, 8, span), f32),
+            pltpu.VMEM((2 * rows, columns), f32),
+            pltpu.VMEM((2 * rows, columns), f32),
+            pltpu.VMEM((2, width + 8, EXTRA), f32),
+            pltpu.VMEM((2, 2, width + 8, EXTRA), f32),
+            pltpu.VMEM((2, span // 128, depth, 128), f32),
+            pltpu.VMEM(half, f32),
+            pltpu.VMEM(half, f32),
+            pltpu.VMEM(half, f32),
+            pltpu.VMEM(half, f32),
+            pltpu.VMEM((2,) + half, f32),
+            dma((rows,)),
+            dma((rows,)),
+            dma,
+            dma,
+            dma((2, 2)),
+            dma((2, 2)),
+            dma((2,)),
+            dma((2,)),
+        ],
+        compiler_params=pltpu.CompilerParams(
+            collective_id=0, has_side_effects=True, vmem_limit_bytes=32 * 1024 * 1024
+        ),
+    )(
+        start_heads,
+        soil_class,
+        soil_conductivity,
+        soil_entry,
+        soil_shape,
+        soil_porosity,
+        emitter_cell.reshape(1, -1),
+        emitter_plan.reshape(1, -1),
+        plan_rates,
+    )
+    return ends.transpose(1, 0, 2)[None]
+
+
 def solution(mesh):
     in_specs = (
         P("cuts", None, "gx", "gy"),
@@ -201,6 +712,9 @@
         P(),
     )
     out_specs = P("cuts", None, "gx", "gy")
+    sizes = mesh.shape
+    fits = sizes["gx"] == 2 and sizes["cuts"] in (4, 8)
+    body = functools.partial(on_pair, sizes) if fits else on_device
     return jax.shard_map(
-        on_device, mesh=mesh, in_specs=in_specs, out_specs=out_specs, check_vma=False
-    )
+        body, mesh=mesh, in_specs=in_specs, out_specs=out_specs, check_vma=False
+    )

time: 303 us -> 28.2 us (0.09)
  the two profiles are of different devices: /device:TPU:16 before, /device:TPU:24 now
where the time goes in v1:
time: 28.2 us; the launch traced here: 28 us
  Pallas kernels  24.9 us (88%)
  local copies, waits for them, and re-layouts  3.04 us (11%)
    pallas_call x1, Pallas kernels, on_pair(): pl.pallas_call(functools.partial(pair_kernel, dict(sizes), width), out_sh...  24.9 us
    unnamed x19, local copies, waits for them, and re-layouts  2.3 us
    broadcast_in_dim x1, local copies, waits for them, and re-layouts, on_pair(): return ends.transpose(1, 0, 2)[None]  0.74 us

profile of v1, /device:TPU:24, one launch (start us, length us, event | category | flops | bytes accessed | tf_op | source)
XLA Modules:
  0.0 28.0 jit_solution(16100370425861639846)
XLA Ops:
  0.0 0.0 copy-start.8
  0.0 0.7 %copy-done.8 = f32[16,4]{0,1:T(4,128)S(1)} copy-done((f32[16,4]{0,1:T(4,128)S(1)}, f32[16,4]{0,1:T(4,128)}, u32[]{:S(2)}) %copy-start.8) | copy-done | bytes 280
  0.7 0.0 copy-start.1
  0.7 0.0 copy-start.2
  0.7 0.0 copy-start.3
  0.7 0.0 copy-start.4
  0.7 0.0 copy-start.5
  0.7 0.0 copy-start.6
  0.7 0.0 copy-start.7
  0.7 0.1 copy.10.rates_ref
  0.8 0.6 %copy-done.1 = s32[4,256]{1,0:T(4,128)S(1)} copy-done((s32[4,256]{1,0:T(4,128)S(1)}, s32[4,256]{1,0:T(4,128)}, u32[]{:S(2)}) %copy-start.1) | copy-done | bytes 4120
  1.4 0.0 copy-done.2
  1.4 0.0 copy-done.3
  1.4 0.0 copy-done.4
  1.4 0.0 copy-done.5
  1.4 0.0 copy-done.6
  1.4 0.0 copy-done.7
  1.4 0.0 copy-start
  1.4 0.9 %copy-done = f32[1,32,4,256]{3,2,1,0:T(4,128)S(1)} copy-done((f32[1,32,4,256]{3,2,1,0:T(4,128)S(1)}, f32[1,32,4,256]{3,2,1,0:T(4,128)}, u32[]{:S(2)}) %copy-start) | copy-done | bytes 131096
  2.3 24.9 %shard_map.91 = f32[4,32,256]{2,1,0:T(8,128)S(1)} custom-call(f32[1,32,4,256]{3,2,1,0:T(4,128)S(1)} %copy-done, s32[4,256]{1,0:T(4,128)S(1)} %copy-done.1, f32[12]{0:T(128)S(1)} %copy-done.4, f32[12]{0:T(128)S(1)} %copy-done.5, f32[12]{0:T(128)S(1)} %copy-done.6, f32[12]{0:T(128)S(1)} %copy-done.7, s32[1,256]{1,0:T(1,128)S(1)} %bitcast.6, ...), custom_call_target="tpu_custom_call" | custom-call | tf_op jit(solution)/shard_map/pallas_call | solution.py:655
  27.3 0.7 %copy.11 = f32[1,32,4,256]{3,2,1,0:T(4,128)} copy(f32[1,32,4,256]{3,1,2,0:T(8,128)S(1)} %bitcast.5) | data formatting | bytes 262144 | tf_op jit(solution)/shard_map/broadcast_in_dim | solution.py:699
Async XLA Ops:
  0.0 0.7 %copy-start.8 = (f32[16,4]{0,1:T(4,128)S(1)}, f32[16,4]{0,1:T(4,128)}, u32[]{:S(2)}) copy-start(f32[16,4]{0,1:T(4,128)} %param.17) | copy-start | bytes 772
  0.7 0.7 %copy-start.1 = (s32[4,256]{1,0:T(4,128)S(1)}, s32[4,256]{1,0:T(4,128)}, u32[]{:S(2)}) copy-start(s32[4,256]{1,0:T(4,128)} %class_ref.1) | copy-start | bytes 12292
  0.7 0.7 %copy-start.2 = (s32[256]{0:T(256)S(1)}, s32[256]{0:T(256)}, u32[]{:S(2)}) copy-start(s32[256]{0:T(256)} %param.15) | copy-start | bytes 3076
  0.7 0.7 %copy-start.3 = (s32[256]{0:T(256)S(1)}, s32[256]{0:T(256)}, u32[]{:S(2)}) copy-start(s32[256]{0:T(256)} %param.16) | copy-start | bytes 3076
  0.7 0.7 %copy-start.4 = (f32[12]{0:T(128)S(1)}, f32[12]{0:T(128)}, u32[]{:S(2)}) copy-start(f32[12]{0:T(128)} %saturated_ref.1) | copy-start | bytes 148
  0.7 0.7 %copy-start.5 = (f32[12]{0:T(128)S(1)}, f32[12]{0:T(128)}, u32[]{:S(2)}) copy-start(f32[12]{0:T(128)} %entry_ref.1) | copy-start | bytes 148
  0.7 0.7 %copy-start.6 = (f32[12]{0:T(128)S(1)}, f32[12]{0:T(128)}, u32[]{:S(2)}) copy-start(f32[12]{0:T(128)} %shape_ref.1) | copy-start | bytes 148
  0.7 0.7 %copy-start.7 = (f32[12]{0:T(128)S(1)}, f32[12]{0:T(128)}, u32[]{:S(2)}) copy-start(f32[12]{0:T(128)} %porosity_ref.1) | copy-start | bytes 148
  1.4 0.9 %copy-start = (f32[1,32,4,256]{3,2,1,0:T(4,128)S(1)}, f32[1,32,4,256]{3,2,1,0:T(4,128)}, u32[]{:S(2)}) copy-start(f32[1,32,4,256]{3,2,1,0:T(4,128)} %heads_ref.1) | copy-start | bytes 393220

commit v2 on v1

--- a/solution.py
+++ b/solution.py
@@ -233,7 +233,7 @@
     return (inflow - outflow) * (1.0 / spacing)
 
 
-def coarse_steps(own, other, params, steps, column_open, even):
+def coarse_steps(own, other, params, steps, column_open, even, both=False):
     wide = 2.0
     pairs = [own, other]
     for s in range(steps):
@@ -245,7 +245,7 @@
         )
         fresh = []
         for w in range(2):
-            if w == 1 and s == steps - 1:
+            if w == 1 and s == steps - 1 and not both:
                 fresh.append(pairs[1])
                 continue
             heads, (half, rate) = pairs[w], closed[w]
@@ -258,7 +258,7 @@
             balance = lateral * (1.0 / (wide * wide)) + vertical(heads, half, params[w][5], wide)
             fresh.append(heads + rate * balance)
         pairs = fresh
-    return pairs[0]
+    return pairs if both else pairs[0]
 
 
 def pair_kernel(
@@ -279,6 +279,7 @@
     speeds,
     table,
     coarse_table,
+    coarse_source,
     aux_out,
     aux_in,
     edge_out,
@@ -286,7 +287,7 @@
     fold,
     old,
     fresh,
-    correction,
+    chained,
     chain_out,
     chain_in,
     row_send,
@@ -306,7 +307,7 @@
     gy = lax.axis_index("gy")
     low = gx == 0
     has_left, has_right = gy > 0, gy < column_tiles - 1
-    has_before, has_after = k > 0, k < slices - 1
+    has_before = k > 0
     pieces = 128 // width
 
     partner = (k, 1 - gx, gy)
@@ -316,10 +317,10 @@
         (has_left, (k, 1 - gx, gy - 1)),
         (has_right, (k, gx, gy + 1)),
         (has_right, (k, 1 - gx, gy + 1)),
-        (has_before, (k - 1, gx, gy)),
-        (has_before, (k - 1, 1 - gx, gy)),
-        (has_after, (k + 1, gx, gy)),
-        (has_after, (k + 1, 1 - gx, gy)),
+    ) + tuple(
+        (None, (lax.rem(k + d, slices), row_half, gy))
+        for d in range(1, slices)
+        for row_half in (gx, 1 - gx)
     )
     barrier = pltpu.get_barrier_semaphore()
     for there, device in greeted:
@@ -341,28 +342,51 @@
         )
 
     kinds = rates_ref.shape[0]
-    picked = lax.broadcasted_iota(jnp.int32, rates_ref.shape, 1) == k
-    rate_of = jnp.sum(jnp.where(picked, rates_ref[...], 0.0), axis=1, keepdims=True)
     plan = plan_ref[...]
     cell = cell_ref[...]
     count = plan.shape[1]
     planned = plan == lax.broadcasted_iota(jnp.int32, (kinds, count), 0)
-    rates = jnp.sum(jnp.where(planned, rate_of, 0.0), axis=0, keepdims=True)
     row_of, column_of = cell // columns, cell % columns
-    line = lax.broadcasted_iota(jnp.int32, (8, count), 0)
+    line = lax.broadcasted_iota(jnp.int32, (slices * rows, count), 0)
+    owner, line = line // rows, line % rows
     line = jnp.where(low, line, rows - 1 - line)
-    by_row = jnp.where(row_of == line, rates, 0.0)
+    by_row = jnp.zeros((slices * rows, count), jnp.float32)
+    for kk in range(slices):
+        rate_of = rates_ref[:, kk : kk + 1]
+        rates = jnp.sum(jnp.where(planned, rate_of, 0.0), axis=0, keepdims=True)
+        by_row = jnp.where(owner == kk, rates, by_row)
+    by_row = jnp.where(row_of == line, by_row, 0.0)
     by_column = jnp.where(
         column_of == lax.broadcasted_iota(jnp.int32, (columns, count), 0), 1.0, 0.0
-    )
-    source = lax.dot_general(
-        by_row,
-        by_column,
-        (((1,), (1,)), ((), ())),
-        precision=lax.Precision.HIGHEST,
-        preferred_element_type=jnp.float32,
-    )
-    aux_out[pl.ds(rows, rows), :] = source[:rows]
+    ).astype(jnp.bfloat16)
+    parts, rest = [], by_row
+    for _ in range(3):
+        parts.append(rest.astype(jnp.bfloat16))
+        rest = rest - parts[-1].astype(jnp.float32)
+    sources = sum(
+        lax.dot_general(
+            part,
+            by_column,
+            (((1,), (1,)), ((), ())),
+            preferred_element_type=jnp.float32,
+        )
+        for part in parts
+    )
+    source = sources[:rows]
+    for kk in range(1, slices):
+        source = jnp.where(k == kk, sources[kk * rows : (kk + 1) * rows], source)
+    aux_out[pl.ds(rows, rows), :] = source
+    even_own = lax.broadcasted_iota(jnp.int32, (1, columns), 1) % 2 == 0
+    for kk in range(slices):
+        at = [sources[kk * rows + j : kk * rows + j + 1] for j in range(rows)]
+        first, second = at[0] + at[1], at[2] + at[3]
+        aux_out[pl.ds(2 * rows + kk, 1), :] = 0.25 * jnp.where(
+            even_own, first + shifted(first, -1, 1), second + shifted(second, 1, 1)
+        )
+    if slices < 8:
+        aux_out[pl.ds(2 * rows + slices, 8 - slices), :] = jnp.zeros(
+            (8 - slices, columns), jnp.float32
+        )
 
     lane = lax.broadcasted_iota(jnp.int32, (width, EXTRA), 1)
     packs = [jnp.zeros((width, EXTRA), jnp.float32) for _ in range(2)]
@@ -375,7 +399,7 @@
             packs[side] = jnp.where(here, shifted(block, (p + side) * width, 1), packs[side])
     for side in range(2):
         edge_out[side, pl.ds(0, width), :] = packs[side]
-        edge_out[side, pl.ds(width, 8), :] = aux_out[:, pl.ds(side * (columns - 128), 128)]
+        edge_out[side, pl.ds(width, 16), :] = aux_out[:, pl.ds(side * (columns - 128), 128)]
 
     def fill(side):
         for who in range(2):
@@ -384,8 +408,8 @@
     pl.when(jnp.logical_not(has_right))(lambda: fill(0))
     pl.when(jnp.logical_not(has_left))(lambda: fill(1))
 
-    sides = [has_left, has_right, has_before, has_after]
-    pl.semaphore_wait(barrier, 1 + 2 * sum(there.astype(jnp.int32) for there in sides))
+    beside = has_left.astype(jnp.int32) + has_right.astype(jnp.int32)
+    pl.semaphore_wait(barrier, 2 * slices - 1 + 2 * beside)
 
     def copy(source_ref, target_ref, send, recv, device):
         return pltpu.make_async_remote_copy(
@@ -451,15 +475,15 @@
             row = j if who == 0 else 2 * rows - 1 - j
             field[0, row, pl.ds(part * width, width), pl.ds(columns, EXTRA)] = block
 
-    third8 = lax.broadcasted_iota(jnp.int32, (8, EXTRA), 1)
+    third8 = lax.broadcasted_iota(jnp.int32, (16, EXTRA), 1)
     wide_aux = [
         jnp.concatenate(
             [
                 (aux_out if who == 0 else aux_in)[...],
                 jnp.where(
                     third8 < EXTRA // 2,
-                    edge_in[0, who, pl.ds(width, 8), :],
-                    edge_in[1, who, pl.ds(width, 8), :],
+                    edge_in[0, who, pl.ds(width, 16), :],
+                    edge_in[1, who, pl.ds(width, 16), :],
                 ),
             ],
             axis=1,
@@ -487,19 +511,20 @@
         means = [
             0.25 * paired(f[0:1] + f[1:2], f[2:3] + f[3:4]) for f in found
         ]
-        spread = 0.25 * paired(
-            src[rows : rows + 1] + src[rows + 1 : rows + 2],
-            src[rows + 2 : rows + 3] + src[rows + 3 : rows + 4],
-        )
-        for i, value in enumerate(derived(*means) + (spread,)):
+        coarse_source[who] = src[2 * rows :]
+        for i, value in enumerate(derived(*means)):
             coarse_table[who, pl.ds(i, 1), :] = value
-        for i, value in enumerate(derived(*[f[:rows] for f in found]) + (src[rows:],)):
+        for i, value in enumerate(derived(*[f[:rows] for f in found]) + (src[rows : 2 * rows],)):
             for j in range(rows):
                 row = j if who == 0 else 2 * rows - 1 - j
                 table[row, pl.ds(i, 1), :] = value[j : j + 1]
 
-    def coarse_params(who):
-        return [coarse_table[who, pl.ds(i, 1), :] for i in range(6)]
+    def coarse_params(kk):
+        return [
+            [coarse_table[who, pl.ds(i, 1), :] for i in range(5)]
+            + [coarse_source[who, pl.ds(kk, 1), :]]
+            for who in range(2)
+        ]
 
     def restricted(slot, row_ids):
         for q in range(2):
@@ -523,7 +548,7 @@
     old[...] = coarse_steps(
         restricted(0, (0, 1, 2, 3)),
         restricted(0, (last, last - 1, last - 2, last - 3)),
-        [coarse_params(0), coarse_params(1)],
+        coarse_params(k),
         COARSE_STEPS,
         coarse_open,
         even,
@@ -564,18 +589,53 @@
         lax.fori_loop(0, reach, move, 0)
 
     done = FINE_STEPS % 2
-    correction[...] = restricted(done, (0, 1, 2, 3)) - old[...]
-
-    chain_copies = [
-        copy(
+    reached = restricted(done, (0, 1, 2, 3))
+    chain_out[...] = (reached - old[...]) + jnp.where(has_before, 0.0, old[...])
+
+    def chain_copy(far, who):
+        return copy(
             chain_out,
-            chain_in.at[who],
-            chain_send.at[who],
-            chain_recv.at[who],
-            (k + 1, gx if who == 0 else 1 - gx, gy),
-        )
-        for who in range(2)
-    ]
+            chain_in.at[k, who],
+            chain_send.at[far - 1, who],
+            chain_recv.at[k, who],
+            (k + far, gx if who == 0 else 1 - gx, gy),
+        )
+
+    def chain_wait(kk):
+        for who in range(2):
+            copy(
+                chain_out,
+                chain_in.at[kk, who],
+                chain_send.at[0, who],
+                chain_recv.at[kk, who],
+                partner,
+            ).wait_recv()
+
+    for far in reversed(range(1, slices)):
+        @pl.when(k + far < slices)
+        def _():
+            for who in range(2):
+                chain_copy(far, who).start()
+
+    for kk in range(slices - 1):
+        @pl.when(k > kk)
+        def _():
+            chain_wait(kk)
+            if kk == 0:
+                for who in range(2):
+                    chained[who] = chain_in[0, who]
+            else:
+                moved = coarse_steps(
+                    chained[0],
+                    chained[1],
+                    coarse_params(kk),
+                    COARSE_STEPS,
+                    coarse_open,
+                    even,
+                    both=True,
+                )
+                for who in range(2):
+                    chained[who] = moved[who] + chain_in[kk, who]
 
     @pl.when(jnp.logical_not(has_before))
     def _():
@@ -583,22 +643,9 @@
 
     @pl.when(has_before)
     def _():
-        for who in range(2):
-            chain_copies[who].wait_recv()
         fresh[...] = coarse_steps(
-            chain_in[0],
-            chain_in[1],
-            [coarse_params(0), coarse_params(1)],
-            COARSE_STEPS,
-            coarse_open,
-            even,
-        )
-
-    @pl.when(has_after)
-    def _():
-        chain_out[...] = fresh[...] + correction[...]
-        for who in range(2):
-            chain_copies[who].start()
+            chained[0], chained[1], coarse_params(k), COARSE_STEPS, coarse_open, even
+        )
 
     change = fresh[...] - old[...]
     spread_rows = (
@@ -626,10 +673,11 @@
             for who in range(2):
                 edge_copies[side][who].wait_send()
 
-    @pl.when(has_after)
-    def _():
-        for who in range(2):
-            chain_copies[who].wait_send()
+    for far in range(1, slices):
+        @pl.when(k + far < slices)
+        def _():
+            for who in range(2):
+                chain_copy(far, who).wait_send()
 
 
 def on_pair(
@@ -663,24 +711,25 @@
             pltpu.VMEM((2 * rows, depth, span), f32),
             pltpu.VMEM((2 * rows, 8, span), f32),
             pltpu.VMEM((2, 8, span), f32),
-            pltpu.VMEM((2 * rows, columns), f32),
-            pltpu.VMEM((2 * rows, columns), f32),
-            pltpu.VMEM((2, width + 8, EXTRA), f32),
-            pltpu.VMEM((2, 2, width + 8, EXTRA), f32),
+            pltpu.VMEM((2, 8, span), f32),
+            pltpu.VMEM((16, columns), f32),
+            pltpu.VMEM((16, columns), f32),
+            pltpu.VMEM((2, width + 16, EXTRA), f32),
+            pltpu.VMEM((2, 2, width + 16, EXTRA), f32),
             pltpu.VMEM((2, span // 128, depth, 128), f32),
             pltpu.VMEM(half, f32),
             pltpu.VMEM(half, f32),
+            pltpu.VMEM((2,) + half, f32),
             pltpu.VMEM(half, f32),
-            pltpu.VMEM(half, f32),
-            pltpu.VMEM((2,) + half, f32),
+            pltpu.VMEM((sizes["cuts"], 2) + half, f32),
             dma((rows,)),
             dma((rows,)),
             dma,
             dma,
             dma((2, 2)),
             dma((2, 2)),
-            dma((2,)),
-            dma((2,)),
+            dma((sizes["cuts"], 2)),
+            dma((sizes["cuts"], 2)),
         ],
         compiler_params=pltpu.CompilerParams(
             collective_id=0, has_side_effects=True, vmem_limit_bytes=32 * 1024 * 1024

time: 28.2 us -> 25.1 us (0.89)
  the two profiles are of different devices: /device:TPU:24 before, /device:TPU:16 now
where the time goes in v2:
time: 25.1 us; the launch traced here: 24.9 us
  Pallas kernels  21.8 us (87%)
  local copies, waits for them, and re-layouts  3.04 us (12%)
    pallas_call x1, Pallas kernels, on_pair(): pl.pallas_call(functools.partial(pair_kernel, dict(sizes), width), out_sh...  21.8 us
    unnamed x19, local copies, waits for them, and re-layouts  2.3 us
    broadcast_in_dim x1, local copies, waits for them, and re-layouts, on_pair(): return ends.transpose(1, 0, 2)[None]  0.74 us

profile of v2, /device:TPU:16, one launch (start us, length us, event | category | flops | bytes accessed | tf_op | source)
XLA Modules:
  0.0 24.9 jit_solution(13400832112198333080)
XLA Ops:
  0.0 0.0 copy-start.8
  0.0 0.7 %copy-done.8 = f32[16,4]{0,1:T(4,128)S(1)} copy-done((f32[16,4]{0,1:T(4,128)S(1)}, f32[16,4]{0,1:T(4,128)}, u32[]{:S(2)}) %copy-start.8) | copy-done | bytes 280
  0.7 0.0 copy-start.1
  0.7 0.0 copy-start.2
  0.7 0.0 copy-start.3
  0.7 0.0 copy-start.4
  0.7 0.0 copy-start.5
  0.7 0.0 copy-start.6
  0.7 0.0 copy-start.7
  0.7 0.1 copy.10.rates_ref
  0.8 0.6 %copy-done.1 = s32[4,256]{1,0:T(4,128)S(1)} copy-done((s32[4,256]{1,0:T(4,128)S(1)}, s32[4,256]{1,0:T(4,128)}, u32[]{:S(2)}) %copy-start.1) | copy-done | bytes 4120
  1.4 0.0 copy-done.2
  1.4 0.0 copy-done.3
  1.4 0.0 copy-done.4
  1.4 0.0 copy-done.5
  1.4 0.0 copy-done.6
  1.4 0.0 copy-done.7
  1.4 0.0 copy-start
  1.4 0.9 %copy-done = f32[1,32,4,256]{3,2,1,0:T(4,128)S(1)} copy-done((f32[1,32,4,256]{3,2,1,0:T(4,128)S(1)}, f32[1,32,4,256]{3,2,1,0:T(4,128)}, u32[]{:S(2)}) %copy-start) | copy-done | bytes 131096
  2.3 21.8 %shard_map.91 = f32[4,32,256]{2,1,0:T(8,128)S(1)} custom-call(f32[1,32,4,256]{3,2,1,0:T(4,128)S(1)} %copy-done, s32[4,256]{1,0:T(4,128)S(1)} %copy-done.1, f32[12]{0:T(128)S(1)} %copy-done.4, f32[12]{0:T(128)S(1)} %copy-done.5, f32[12]{0:T(128)S(1)} %copy-done.6, f32[12]{0:T(128)S(1)} %copy-done.7, s32[1,256]{1,0:T(1,128)S(1)} %bitcast.6, ...), custom_call_target="tpu_custom_call" | custom-call | tf_op jit(solution)/shard_map/pallas_call | solution.py:703
  24.1 0.7 %copy.11 = f32[1,32,4,256]{3,2,1,0:T(4,128)} copy(f32[1,32,4,256]{3,1,2,0:T(8,128)S(1)} %bitcast.5) | data formatting | bytes 262144 | tf_op jit(solution)/shard_map/broadcast_in_dim | solution.py:748
Async XLA Ops:
  0.0 0.7 %copy-start.8 = (f32[16,4]{0,1:T(4,128)S(1)}, f32[16,4]{0,1:T(4,128)}, u32[]{:S(2)}) copy-start(f32[16,4]{0,1:T(4,128)} %param.17) | copy-start | bytes 772
  0.7 0.7 %copy-start.1 = (s32[4,256]{1,0:T(4,128)S(1)}, s32[4,256]{1,0:T(4,128)}, u32[]{:S(2)}) copy-start(s32[4,256]{1,0:T(4,128)} %class_ref.1) | copy-start | bytes 12292
  0.7 0.7 %copy-start.2 = (s32[256]{0:T(256)S(1)}, s32[256]{0:T(256)}, u32[]{:S(2)}) copy-start(s32[256]{0:T(256)} %param.15) | copy-start | bytes 3076
  0.7 0.7 %copy-start.3 = (s32[256]{0:T(256)S(1)}, s32[256]{0:T(256)}, u32[]{:S(2)}) copy-start(s32[256]{0:T(256)} %param.16) | copy-start | bytes 3076
  0.7 0.7 %copy-start.4 = (f32[12]{0:T(128)S(1)}, f32[12]{0:T(128)}, u32[]{:S(2)}) copy-start(f32[12]{0:T(128)} %saturated_ref.1) | copy-start | bytes 148
  0.7 0.7 %copy-start.5 = (f32[12]{0:T(128)S(1)}, f32[12]{0:T(128)}, u32[]{:S(2)}) copy-start(f32[12]{0:T(128)} %entry_ref.1) | copy-start | bytes 148
  0.7 0.7 %copy-start.6 = (f32[12]{0:T(128)S(1)}, f32[12]{0:T(128)}, u32[]{:S(2)}) copy-start(f32[12]{0:T(128)} %shape_ref.1) | copy-start | bytes 148
  0.7 0.7 %copy-start.7 = (f32[12]{0:T(128)S(1)}, f32[12]{0:T(128)}, u32[]{:S(2)}) copy-start(f32[12]{0:T(128)} %porosity_ref.1) | copy-start | bytes 148
  1.4 0.9 %copy-start = (f32[1,32,4,256]{3,2,1,0:T(4,128)S(1)}, f32[1,32,4,256]{3,2,1,0:T(4,128)}, u32[]{:S(2)}) copy-start(f32[1,32,4,256]{3,2,1,0:T(4,128)} %heads_ref.1) | copy-start | bytes 393220

commit v3 on v2

--- a/solution.py
+++ b/solution.py
@@ -264,7 +264,16 @@
 def pair_kernel(
     sizes,
     width,
-    heads_ref,
+    heads_hbm,
+    class_hbm,
+    saturated_hbm,
+    entry_hbm,
+    shape_hbm,
+    porosity_hbm,
+    cell_hbm,
+    plan_hbm,
+    rates_hbm,
+    out_ref,
     class_ref,
     saturated_ref,
     entry_ref,
@@ -273,7 +282,7 @@
     cell_ref,
     plan_ref,
     rates_ref,
-    out_ref,
+    load_sem,
     field,
     halves,
     speeds,
@@ -300,7 +309,7 @@
     chain_recv,
 ):
     slices, column_tiles = sizes["cuts"], sizes["gy"]
-    _, depth, rows, columns = heads_ref.shape
+    _, depth, rows, columns = heads_hbm.shape
     span = columns + EXTRA
     k = lax.axis_index("cuts")
     gx = lax.axis_index("gx")
@@ -332,29 +341,53 @@
         else:
             pl.when(there)(greet)
 
-    own = [heads_ref[0, :, r, :] for r in range(rows)]
-    for j in range(rows):
-        field[0, j, :, pl.ds(0, columns)] = jnp.where(low, own[j], own[rows - 1 - j])
+    loads = [
+        pltpu.make_async_copy(
+            heads_hbm.at[0, :, r, :],
+            field.at[0, jnp.where(low, r, rows - 1 - r), :, pl.ds(0, columns)],
+            load_sem.at[r],
+        )
+        for r in range(rows)
+    ]
+    small = [
+        pltpu.make_async_copy(there, here, load_sem.at[rows + i])
+        for i, (there, here) in enumerate(
+            (
+                (class_hbm, class_ref),
+                (cell_hbm, cell_ref),
+                (plan_hbm, plan_ref),
+                (rates_hbm, rates_ref),
+                (saturated_hbm, saturated_ref),
+                (entry_hbm, entry_ref),
+                (shape_hbm, shape_ref),
+                (porosity_hbm, porosity_ref),
+            )
+        )
+    ]
+    for load in small + loads:
+        load.start()
+    for load in small:
+        load.wait()
     classes = class_ref[...].astype(jnp.float32)
     for j in range(rows):
         aux_out[pl.ds(j, 1), :] = jnp.where(
             low, classes[j : j + 1], classes[rows - 1 - j : rows - j]
         )
 
-    kinds = rates_ref.shape[0]
+    kinds = rates_ref.shape[1]
     plan = plan_ref[...]
     cell = cell_ref[...]
     count = plan.shape[1]
-    planned = plan == lax.broadcasted_iota(jnp.int32, (kinds, count), 0)
+    rates_all = jnp.zeros((slices, count), jnp.float32)
+    for kind in range(kinds):
+        rates_all = jnp.where(plan == kind, rates_ref[:, kind : kind + 1], rates_all)
     row_of, column_of = cell // columns, cell % columns
     line = lax.broadcasted_iota(jnp.int32, (slices * rows, count), 0)
     owner, line = line // rows, line % rows
     line = jnp.where(low, line, rows - 1 - line)
     by_row = jnp.zeros((slices * rows, count), jnp.float32)
     for kk in range(slices):
-        rate_of = rates_ref[:, kk : kk + 1]
-        rates = jnp.sum(jnp.where(planned, rate_of, 0.0), axis=0, keepdims=True)
-        by_row = jnp.where(owner == kk, rates, by_row)
+        by_row = jnp.where(owner == kk, rates_all[kk : kk + 1], by_row)
     by_row = jnp.where(row_of == line, by_row, 0.0)
     by_column = jnp.where(
         column_of == lax.broadcasted_iota(jnp.int32, (columns, count), 0), 1.0, 0.0
@@ -388,6 +421,8 @@
             (8 - slices, columns), jnp.float32
         )
 
+    for load in loads:
+        load.wait()
     lane = lax.broadcasted_iota(jnp.int32, (width, EXTRA), 1)
     packs = [jnp.zeros((width, EXTRA), jnp.float32) for _ in range(2)]
     per_row = depth // width
@@ -561,20 +596,20 @@
         now, later = s % 2, (s + 1) % 2
         reach = 2 * rows - 1 - s
 
-        def close(j, carry):
+        def close(j):
             given = [table[j, pl.ds(i, 1), :] for i in range(5)]
             half, rate = closure(field[now, j], *given, 1.0)
             halves[j] = half
             speeds[j] = rate
-            return carry
-
-        lax.fori_loop(0, reach + 1, close, 0)
-
-        def move(j, carry):
+
+        for j in range(reach + 1):
+            close(j)
+
+        def move(j):
             heads, half = field[now, j], halves[j]
             right = fine_open * (half + shifted(half, -1, 1)) * (shifted(heads, -1, 1) - heads)
             up = (half + halves[j + 1]) * (field[now, j + 1] - heads)
-            before = jnp.maximum(j - 1, 0)
+            before = max(j - 1, 0)
             down = (half + halves[before]) * (field[now, before] - heads)
             balance = (
                 right
@@ -584,9 +619,9 @@
                 + vertical(heads, half, table[j, pl.ds(5, 1), :], 1.0)
             )
             field[later, j] = heads + speeds[j] * balance
-            return carry
-
-        lax.fori_loop(0, reach, move, 0)
+
+        for j in range(reach):
+            move(j)
 
     done = FINE_STEPS % 2
     reached = restricted(done, (0, 1, 2, 3))
@@ -614,7 +649,7 @@
     for far in reversed(range(1, slices)):
         @pl.when(k + far < slices)
         def _():
-            for who in range(2):
+            for who in (1, 0):
                 chain_copy(far, who).start()
 
     for kk in range(slices - 1):
@@ -696,16 +731,26 @@
     span = columns + EXTRA
     width = 4 * sizes["cuts"]
     vmem = pl.BlockSpec(memory_space=pltpu.VMEM)
-    smem = pl.BlockSpec(memory_space=pltpu.SMEM)
+    classes = soil_conductivity.shape
+    emitters = (1, emitter_cell.shape[0])
     dma = pltpu.SemaphoreType.DMA
     f32 = jnp.float32
     half = (depth // 2, span)
     ends = pl.pallas_call(
         functools.partial(pair_kernel, dict(sizes), width),
         out_shape=jax.ShapeDtypeStruct((rows, depth, columns), f32),
-        in_specs=[vmem, vmem, smem, smem, smem, smem, vmem, vmem, vmem],
+        in_specs=[pl.BlockSpec(memory_space=pltpu.HBM)] * 9,
         out_specs=vmem,
         scratch_shapes=[
+            pltpu.VMEM((rows, columns), jnp.int32),
+            pltpu.SMEM(classes, f32),
+            pltpu.SMEM(classes, f32),
+            pltpu.SMEM(classes, f32),
+            pltpu.SMEM(classes, f32),
+            pltpu.VMEM(emitters, jnp.int32),
+            pltpu.VMEM(emitters, jnp.int32),
+            pltpu.VMEM(plan_rates.shape[::-1], f32),
+            dma((rows + 8,)),
             pltpu.VMEM((2, 2 * rows, depth, span), f32),
             pltpu.VMEM((2 * rows, depth, span), f32),
             pltpu.VMEM((2 * rows, depth, span), f32),
@@ -732,7 +777,7 @@
             dma((sizes["cuts"], 2)),
         ],
         compiler_params=pltpu.CompilerParams(
-            collective_id=0, has_side_effects=True, vmem_limit_bytes=32 * 1024 * 1024
+            collective_id=0, has_side_effects=True, vmem_limit_bytes=60 * 1024 * 1024
         ),
     )(
         start_heads,
@@ -743,7 +788,7 @@
         soil_porosity,
         emitter_cell.reshape(1, -1),
         emitter_plan.reshape(1, -1),
-        plan_rates,
+        plan_rates.T,
     )
     return ends.transpose(1, 0, 2)[None]
 

time: 25.1 us -> 20.3 us (0.81)
  Pallas kernels: 21.8 us -> 18.4 us
  local copies, waits for them, and re-layouts: 3.04 us -> 1.65 us
    pallas_call x1, Pallas kernels: 21.8 us -> 18.4 us  [on_pair(): pl.pallas_call(functools.partial(pair_kernel, dict(sizes), width), out_sh...]
    unnamed x19 -> x0, local copies, waits for them, and re-layouts: 2.3 us -> none
    broadcast_in_dim x1, local copies, waits for them, and re-layouts: 0.74 us -> 1.65 us  [on_pair(): return ends.transpose(1, 0, 2)[None]]
where the time goes in v3:
time: 20.3 us; the launch traced here: 20.1 us
  Pallas kernels  18.4 us (91%)
  local copies, waits for them, and re-layouts  1.65 us (8%)
    pallas_call x1, Pallas kernels, on_pair(): pl.pallas_call(functools.partial(pair_kernel, dict(sizes), width), out_sh...  18.4 us
    broadcast_in_dim x1, local copies, waits for them, and re-layouts, on_pair(): return ends.transpose(1, 0, 2)[None]  1.65 us

profile of v3, /device:TPU:16, one launch (start us, length us, event | category | flops | bytes accessed | tf_op | source)
XLA Modules:
  0.0 20.1 jit_solution(10673291527918797464)
XLA Ops:
  0.0 18.4 %shard_map.91 = f32[4,32,256]{2,1,0:T(8,128)} custom-call(f32[1,32,4,256]{3,2,1,0:T(4,128)} %heads_hbm.1, s32[4,256]{1,0:T(4,128)} %class_hbm.1, f32[12]{0:T(128)} %saturated_hbm.1, f32[12]{0:T(128)} %entry_hbm.1, f32[12]{0:T(128)} %shape_hbm.1, f32[12]{0:T(128)} %porosity_hbm.1, s32[1,256]{1,0:T(1,128)} %bitcast.8, s32[1,256]{1,0:T(1,128)} %bitcast.9, ...), custom_call_target="tpu_custom_call" | custom-call | tf_op jit(solution)/shard_map/pallas_call | solution.py:739
  18.4 1.6 %copy.10 = f32[1,32,4,256]{3,2,1,0:T(4,128)} copy(f32[1,32,4,256]{3,1,2,0:T(8,128)} %bitcast.6) | data formatting | bytes 262144 | tf_op jit(solution)/shard_map/broadcast_in_dim | solution.py:793

commit v4 on v3

--- a/solution.py
+++ b/solution.py
@@ -576,22 +576,7 @@
             sums.append(jnp.concatenate(lines, axis=1))
         return 0.125 * paired(*sums)
 
-    for j in reversed(range(rows)):
-        row_copies[j].wait_recv()
-
     last = 2 * rows - 1
-    old[...] = coarse_steps(
-        restricted(0, (0, 1, 2, 3)),
-        restricted(0, (last, last - 1, last - 2, last - 3)),
-        coarse_params(k),
-        COARSE_STEPS,
-        coarse_open,
-        even,
-    )
-
-    for j in range(rows):
-        row_copies[j].wait_send()
-
     for s in range(FINE_STEPS):
         now, later = s % 2, (s + 1) % 2
         reach = 2 * rows - 1 - s
@@ -603,6 +588,8 @@
             speeds[j] = rate
 
         for j in range(reach + 1):
+            if s == 0 and j >= rows:
+                row_copies[2 * rows - 1 - j].wait_recv()
             close(j)
 
         def move(j):
@@ -620,12 +607,18 @@
             )
             field[later, j] = heads + speeds[j] * balance
 
+        if s == 1:
+            for j in range(rows):
+                row_copies[j].wait_send()
         for j in range(reach):
             move(j)
+        if s == 0:
+            chained[0] = restricted(0, (0, 1, 2, 3))
+            chained[1] = restricted(0, (last, last - 1, last - 2, last - 3))
+
 
     done = FINE_STEPS % 2
     reached = restricted(done, (0, 1, 2, 3))
-    chain_out[...] = (reached - old[...]) + jnp.where(has_before, 0.0, old[...])
 
     def chain_copy(far, who):
         return copy(
@@ -646,8 +639,23 @@
                 partner,
             ).wait_recv()
 
+    @pl.when(jnp.logical_not(has_before))
+    def _():
+        chain_out[...] = reached
+        for far in reversed(range(1, slices)):
+            for who in (1, 0):
+                chain_copy(far, who).start()
+
+    old[...] = coarse_steps(
+        chained[0], chained[1], coarse_params(k), COARSE_STEPS, coarse_open, even
+    )
+
+    @pl.when(has_before)
+    def _():
+        chain_out[...] = reached - old[...]
+
     for far in reversed(range(1, slices)):
-        @pl.when(k + far < slices)
+        @pl.when(has_before & (k + far < slices))
         def _():
             for who in (1, 0):
                 chain_copy(far, who).start()

time: 20.3 us -> 20.3 us (level)
  no operation moved by 1% of the time
where the time goes in v4:
time: 20.3 us; the launch traced here: 20.1 us
  Pallas kernels  18.4 us (91%)
  local copies, waits for them, and re-layouts  1.65 us (8%)
    pallas_call x1, Pallas kernels, on_pair(): pl.pallas_call(functools.partial(pair_kernel, dict(sizes), width), out_sh...  18.4 us
    broadcast_in_dim x1, local copies, waits for them, and re-layouts, on_pair(): return ends.transpose(1, 0, 2)[None]  1.65 us

profile of v4, /device:TPU:16, one launch (start us, length us, event | category | flops | bytes accessed | tf_op | source)
XLA Modules:
  0.0 20.1 jit_solution(8580181469215962461)
XLA Ops:
  0.0 18.4 %shard_map.91 = f32[4,32,256]{2,1,0:T(8,128)} custom-call(f32[1,32,4,256]{3,2,1,0:T(4,128)} %heads_hbm.1, s32[4,256]{1,0:T(4,128)} %class_hbm.1, f32[12]{0:T(128)} %saturated_hbm.1, f32[12]{0:T(128)} %entry_hbm.1, f32[12]{0:T(128)} %shape_hbm.1, f32[12]{0:T(128)} %porosity_hbm.1, s32[1,256]{1,0:T(1,128)} %bitcast.8, s32[1,256]{1,0:T(1,128)} %bitcast.9, ...), custom_call_target="tpu_custom_call" | custom-call | tf_op jit(solution)/shard_map/pallas_call | solution.py:747
  18.4 1.6 %copy.10 = f32[1,32,4,256]{3,2,1,0:T(4,128)} copy(f32[1,32,4,256]{3,1,2,0:T(8,128)} %bitcast.6) | data formatting | bytes 262144 | tf_op jit(solution)/shard_map/broadcast_in_dim | solution.py:801
